TPU v7x, 256 devices: a whole 4x4x8 slice. The times are simulated.
256 devices in a mesh: dom: 64 (over y, z, core), sub: 4 (over x).
Axes of the slice: x: 4, y: 4, z: 8, core: 2. Of those that a mesh axis runs over, the one named last changes fastest.
Arguments:
- features: bfloat16 [262144, 128], P(('dom', 'sub')), may hold values from -6 to 6
- weight: bfloat16 [128, 128], replicated, may hold values from -0.5 to 0.5
- layer_bias: float32 [128], replicated, may hold values from -3 to 3
- local_rows: int32 [24576], P(('dom', 'sub')), may hold values from 0 to 7, as said below
- local_blocks: int32 [24576], P(('dom', 'sub')), may hold values from 0 to 7, as said below
- local_values: bfloat16 [24576, 128, 128], P(('dom', 'sub')), may hold values from -0.09375 to 0.09375
- send_rows: int32 [65536, 12], P(('dom', 'sub')), may hold values from 0 to 1023
- bound_rows: int32 [24576], P(('dom', 'sub')), may hold values from 0 to 7, as said below
- bound_blocks: int32 [24576], P(('dom', 'sub')), may hold values from 0 to 23, as said below
- bound_values: bfloat16 [24576, 128, 128], P(('dom', 'sub')), may hold values from -0.09375 to 0.09375
- hub_rows: int32 [2048], P(('dom', 'sub')), may hold values from 0 to 1023
- hub_weights: bfloat16 [262144, 2048], P(('dom', 'sub')), may hold values from -0.078125 to 0.078125
Outputs:
- activated: bfloat16 [262144, 128], P(('dom', 'sub'))
Inputs may be any that keep to these rules, and one draw needn't show every extreme that they name: `local_rows`: each device's 96 entries name every row tile of its nodes at least once. `local_blocks`: each device's entries name every block of 128 of its own nodes at least once; a pair of row tile and block may repeat. `bound_rows`: each device's 96 entries name every row tile of its nodes at least once. `bound_blocks`: each device's entries name every block of 128 received rows at least once; a pair may repeat.
All inputs are finite; a program needn't handle non-finite values.
Results may differ from a plain program's by a relative error of at most 0.0045.
Values may be sent and summed in bfloat16 or wider, within the bound.
No kernel may reach another device: no remote copies, remote signals or barrier semaphores. Data moves between devices by JAX's collectives and lax.ppermute only.
A program may use at most 128 MiB of HBM per device.

v0:
```python
import jax
import jax.numpy as jnp
from jax import lax
from jax.sharding import PartitionSpec as P


def tile_sum(rows_of, blocks_of, values, source, row_tiles):
    tile_size = values.shape[1]
    out_width = source.shape[1]
    blocks = source.reshape(-1, tile_size, out_width)[blocks_of]
    products = jnp.einsum("tij,tjh->tih", values, blocks, preferred_element_type=jnp.float32)
    summed = jnp.zeros((row_tiles, tile_size, out_width), jnp.float32).at[rows_of].add(products)
    return summed.reshape(row_tiles * tile_size, out_width)


def on_device(
    features,
    weight,
    layer_bias,
    local_rows,
    local_blocks,
    local_values,
    send_rows,
    bound_rows,
    bound_blocks,
    bound_values,
    hub_rows,
    hub_weights,
):
    row_tiles = features.shape[0] // local_values.shape[1]
    dom_count = lax.axis_size("dom")
    sub_count = lax.axis_size("sub")
    slot_rows = send_rows.shape[1]
    width = weight.shape[1]
    mapped = jnp.dot(features, weight, preferred_element_type=jnp.float32).astype(jnp.bfloat16)
    boundary_out = mapped[send_rows.reshape(-1)].reshape(dom_count, sub_count, slot_rows, width)
    hub_here = mapped[hub_rows]
    arrived = lax.all_to_all(
        lax.all_to_all(boundary_out, "dom", split_axis=0, concat_axis=0, tiled=True),
        "sub",
        split_axis=1,
        concat_axis=1,
        tiled=True,
    )
    received = arrived.reshape(-1, width)
    hub_part = jnp.dot(
        hub_weights,
        lax.all_gather(hub_here, ("dom", "sub"), axis=0, tiled=True),
        preferred_element_type=jnp.float32,
    )
    local_part = tile_sum(local_rows, local_blocks, local_values, mapped, row_tiles)
    bound_part = tile_sum(bound_rows, bound_blocks, bound_values, received, row_tiles)
    pre_act = local_part + bound_part + hub_part + layer_bias[None, :]
    return jax.nn.relu(pre_act).astype(jnp.bfloat16)


def solution(mesh):
    in_specs = (
        P(("dom", "sub"), None),
        P(),
        P(),
        P(("dom", "sub")),
        P(("dom", "sub")),
        P(("dom", "sub"), None, None),
        P(("dom", "sub"), None),
        P(("dom", "sub")),
        P(("dom", "sub")),
        P(("dom", "sub"), None, None),
        P(("dom", "sub")),
        P(("dom", "sub"), None),
    )
    out_specs = P(("dom", "sub"), None)
    return jax.shard_map(
        on_device, mesh=mesh, in_specs=in_specs, out_specs=out_specs, check_vma=False
    )
```

profile of v0, /device:TPU:1, one launch (start us, length us, event | category | flops | bytes accessed | tf_op | source)
XLA Modules:
  0.0 257.4 jit_solution(16503203828714777169)
XLA Ops:
  0.0 1.0 copy.26
  1.0 0.1 reshape.42
  1.1 1.2 convolution_convert_fusion
  2.3 11.4 %gather_fusion.1 = bf16[3072,128]{1,0:T(8,128)(2,1)} fusion(bf16[1024,128]{1,0:T(8,128)(2,1)S(1)} %convolution_convert_fusion, s32[3072]{0:T(1024)S(1)} %broadcast_clamp_fusion), kind=kCustom, calls=%fused_computation.1 | custom fusion | bytes 1585152 | tf_op jit(solution)/shard_map/gather | solution.py:36
  13.8 2.1 reshape.43
  15.9 2.4 copy.27
  18.3 13.3 %all-to-all-start = ((bf16[64,4,12,128]{3,1,2,0:T(4,128)(2,1)}), bf16[64,4,12,128]{3,1,2,0:T(4,128)(2,1)}, u32[]{:S(2)}, u32[]{:S(2)}) async-start(bf16[64,4,12,128]{3,1,2,0:T(4,128)(2,1)} %copy.27), calls=%async_computation | async-start | bytes 1572864 | tf_op jit(solution)/shard_map/all_to_all | solution.py:39
  31.6 0.0 copy-done.2
  31.6 2.7 %gather_fusion = bf16[96,128,128]{2,1,0:T(8,128)(2,1)} fusion(bf16[8,128,128]{2,1,0:T(8,128)(2,1)S(1)} %bitcast.25, s32[1024]{0:T(1024)S(1)} %pad_clamp_fusion.2), kind=kCustom, calls=%fused_computation | custom fusion | bytes 6291840 | tf_op jit(solution)/shard_map/gather | solution.py:10
  34.3 6.9 %convolution_bitcast_fusion.1 = f32[96,128,128]{1,2,0:T(8,128)} fusion(bf16[96,128,128]{2,1,0:T(8,128)(2,1)} %gather_fusion, bf16[96,128,128]{2,1,0:T(8,128)(2,1)S(1)} %copy-done), kind=kOutput, calls=%fused_computation.7 | convolution fusion | flops 402653184 | bytes 12582912 | tf_op jit(solution)/shard_map/tij,tjh->tih/dot_general | solution.py:11
  41.2 6.6 %copy.25 = f32[96,128,128]{2,1,0:T(8,128)} copy(f32[96,128,128]{1,2,0:T(8,128)} %convolution_bitcast_fusion.1) | data formatting | bytes 12582912 | tf_op jit(solution)/shard_map/tij,tjh->tih/dot_general | solution.py:11
  47.8 0.6 gather_fusion.3
  48.4 0.0 copy-done.4
  48.4 0.8 broadcast.30.clone
  49.2 19.4 %scatter_fusion = f32[8,128,128]{2,1,0:T(8,128)} fusion(f32[8,128,128]{2,1,0:T(8,128)} %broadcast.30.clone, s32[96]{0:T(128)S(1)} %compare_select_fusion.5, f32[96,128,128]{2,1,0:T(8,128)} %copy.25), kind=kCustom, calls=%fused_computation.4 | custom fusion | flops 1572864 | bytes 18874752 | tf_op jit(solution)/shard_map/scatter-add | solution.py:12
  68.6 0.0 copy-done.5
  68.6 0.0 all-to-all-done
  68.6 2.2 copy.28
  70.8 4.2 %all-to-all-start.1 = ((bf16[64,4,12,128]{3,0,2,1:T(8,128)(2,1)}), bf16[64,4,12,128]{3,0,2,1:T(8,128)(2,1)}, u32[]{:S(2)}, u32[]{:S(2)}) async-start(bf16[64,4,12,128]{3,0,2,1:T(8,128)(2,1)} %copy.28), calls=%async_computation.1 | async-start | bytes 1572864 | tf_op jit(solution)/shard_map/all_to_all | solution.py:38
  75.1 130.1 %all-gather = bf16[2048,128]{1,0:T(8,128)(2,1)} all-gather(bf16[8,128]{1,0:T(8,128)(2,1)S(1)} %gather_fusion.3), channel_id=2, replica_groups=mesh['dom'=64,'sub'=4] {'dom','sub'}, dimensions={0}, use_global_device_ids=true | all-gather | bytes 526336 | tf_op jit(solution)/shard_map/all_gather | solution.py:48
  205.2 0.0 all-to-all-done.1
  205.2 2.7 %copy.29 = bf16[64,4,12,128]{3,2,1,0:T(8,128)(2,1)} copy(bf16[64,4,12,128]{3,0,2,1:T(8,128)(2,1)} %all-to-all-done.1) | data formatting | bytes 1572864 | tf_op jit(solution)/shard_map/all_to_all | solution.py:38
  207.8 2.1 reshape_reshape.3
  209.9 3.8 %gather_fusion.2 = bf16[96,128,128]{2,1,0:T(8,128)(2,1)} fusion(bf16[24,128,128]{2,1,0:T(8,128)(2,1)} %reshape_reshape.3, s32[1024]{0:T(1024)S(1)} %pad_clamp_fusion.1), kind=kCustom, calls=%fused_computation.2 | custom fusion | bytes 6291840 | tf_op jit(solution)/shard_map/gather | solution.py:10
  213.7 7.8 %convolution_bitcast_fusion = f32[96,128,128]{1,2,0:T(8,128)} fusion(bf16[96,128,128]{2,1,0:T(8,128)(2,1)} %gather_fusion.2, bf16[96,128,128]{2,1,0:T(8,128)(2,1)} %param.21), kind=kOutput, calls=%fused_computation.6 | convolution fusion | flops 402653184 | bytes 12582912 | tf_op jit(solution)/shard_map/tij,tjh->tih/dot_general | solution.py:11
  221.6 6.6 %copy.31 = f32[96,128,128]{2,1,0:T(8,128)} copy(f32[96,128,128]{1,2,0:T(8,128)} %convolution_bitcast_fusion) | data formatting | bytes 12582912 | tf_op jit(solution)/shard_map/tij,tjh->tih/dot_general | solution.py:11
  228.1 0.9 broadcast.30.clone.1
  229.0 19.5 %scatter_fusion.1 = f32[8,128,128]{2,1,0:T(8,128)} fusion(f32[8,128,128]{2,1,0:T(8,128)} %broadcast.30.clone.1, s32[96]{0:T(128)S(1)} %compare_select_fusion.3, f32[96,128,128]{2,1,0:T(8,128)} %copy.31), kind=kCustom, calls=%fused_computation.5 | custom fusion | flops 1572864 | bytes 18874752 | tf_op jit(solution)/shard_map/scatter-add | solution.py:12
  248.5 2.0 add.59
  250.5 2.0 copy.36
  252.6 4.0 %fusion.3 = bf16[1024,128]{0,1:T(8,128)(2,1)S(1)} fusion(f32[1024,128]{0,1:T(8,128)} %copy.36, bf16[2048,128]{1,0:T(8,128)(2,1)} %all-gather, bf16[1024,2048]{1,0:T(8,128)(2,1)} %param.23, f32[128]{0:T(128)S(1)} %copy-done.1), kind=kOutput, calls=%fused_computation.12 | convolution fusion | flops 537395200 | bytes 5505536 | tf_op jit(solution)/shard_map/dot_general | solution.py:46
  256.6 0.8 copy.33
  (21 shorter events, 0.1 us)
Async XLA Ops:
  0.0 34.3 %copy-start = (bf16[96,128,128]{2,1,0:T(8,128)(2,1)S(1)}, bf16[96,128,128]{2,1,0:T(8,128)(2,1)}, u32[]{:S(2)}) copy-start(bf16[96,128,128]{2,1,0:T(8,128)(2,1)} %param.17) | copy-start | bytes 9437188
  13.8 17.8 %copy-start.2 = (s32[96]{0:T(128)S(1)}, s32[96]{0:T(128)}, u32[]{:S(2)}) copy-start(s32[96]{0:T(128)} %param.16) | copy-start | bytes 1156
  18.3 50.3 %all-to-all-start = ((bf16[64,4,12,128]{3,1,2,0:T(4,128)(2,1)}), bf16[64,4,12,128]{3,1,2,0:T(4,128)(2,1)}, u32[]{:S(2)}, u32[]{:S(2)}) async-start(bf16[64,4,12,128]{3,1,2,0:T(4,128)(2,1)} %copy.27), calls=%async_computation | async-start | bytes 1572864 | tf_op jit(solution)/shard_map/all_to_all | solution.py:39
  41.2 6.6 %copy-start.3 = (s32[8]{0:T(128)S(1)}, s32[8]{0:T(128)}, u32[]{:S(2)}) copy-start(s32[8]{0:T(128)} %param.22) | copy-start | bytes 100
  41.2 7.2 %copy-start.4 = (s32[96]{0:T(128)S(1)}, s32[96]{0:T(128)}, u32[]{:S(2)}) copy-start(s32[96]{0:T(128)} %param.15) | copy-start | bytes 1156
  49.2 19.4 %copy-start.5 = (s32[96]{0:T(128)S(1)}, s32[96]{0:T(128)}, u32[]{:S(2)}) copy-start(s32[96]{0:T(128)} %param.20) | copy-start | bytes 1156
  68.6 6.5 %copy-start.6 = (s32[96]{0:T(128)S(1)}, s32[96]{0:T(128)}, u32[]{:S(2)}) copy-start(s32[96]{0:T(128)} %param.19) | copy-start | bytes 1156
  70.8 134.3 %all-to-all-start.1 = ((bf16[64,4,12,128]{3,0,2,1:T(8,128)(2,1)}), bf16[64,4,12,128]{3,0,2,1:T(8,128)(2,1)}, u32[]{:S(2)}, u32[]{:S(2)}) async-start(bf16[64,4,12,128]{3,0,2,1:T(8,128)(2,1)} %copy.28), calls=%async_computation.1 | async-start | bytes 1572864 | tf_op jit(solution)/shard_map/all_to_all | solution.py:38
  229.0 23.6 %copy-start.1 = (f32[128]{0:T(128)S(1)}, f32[128]{0:T(128)}, u32[]{:S(2)}) copy-start(f32[128]{0:T(128)} %param.14) | copy-start | bytes 1540
where the time goes:
time: 259 us; the launch traced here: 257 us
  blocking collectives  130 us (50%)
  local copies, waits for them, and re-layouts  48.8 us (19%)
  other arithmetic  41 us (16%)
  matrix products  19.9 us (8%)
  starting transfers between devices  17.5 us (7%)
    all_gather x1, blocking collectives, on_device(): lax.all_gather(hub_here, ('dom', 'sub'), axis=0, tiled=True)  130 us
    scatter-add x2, other arithmetic, tile_sum(): jnp.zeros((row_tiles, tile_size, out_width), jnp.float32).at[rows_of]  38.9 us
    dot_general x2, matrix products, tile_sum(): jnp.einsum('tij,tjh->tih', values, blocks, preferred_element_type=jnp.flo...  14.7 us
    all_to_all x1, starting transfers between devices, on_device(): lax.all_to_all(boundary_out, 'dom', split_axis=0, concat_axis=0, tiled=True)  13.3 us
    dot_general x2, local copies, waits for them, and re-layouts, tile_sum(): jnp.einsum('tij,tjh->tih', values, blocks, preferred_element_type=jnp.flo...  13.2 us
    gather x1, local copies, waits for them, and re-layouts, on_device(): mapped[send_rows.reshape(-1)]  11.4 us
    gather x2, local copies, waits for them, and re-layouts, tile_sum(): blocks = source.reshape(-1, tile_size, out_width)[blocks_of]  6.55 us
  transfers between devices with their start and end apart: 2, of which 0 were waited for; matrix products, arithmetic and copies ran while one was open for 14% of the time, Pallas kernels for 0%

commit v1 on v0

v1 whole, which is shorter than its diff:
```python
import functools

import jax
import jax.numpy as jnp
from jax import lax
from jax.experimental import pallas as pl
from jax.experimental.pallas import tpu as pltpu
from jax.sharding import PartitionSpec as P

VMEM = pl.BlockSpec(memory_space=pltpu.VMEM)
SMEM = pl.BlockSpec(memory_space=pltpu.SMEM)
MIB = 1024 * 1024
Y, Z, CORES, X = 4, 8, 2, 4


def send_kernel(slot, send_ref, hub_ref, feat_ref, weight_ref, mapped_ref, out_ref, hub_out_ref, table, stage):
    mapped = jnp.dot(feat_ref[...], weight_ref[...], preferred_element_type=jnp.float32)
    mapped = mapped.astype(jnp.bfloat16)
    mapped_ref[...] = mapped
    table[...] = mapped.astype(jnp.float32)
    receivers = send_ref.shape[1]

    hub_rows = [table[pl.ds(hub_ref[j], 1), :] for j in range(hub_ref.shape[0])]
    hub_out_ref[...] = jnp.concatenate(hub_rows, axis=0).astype(jnp.bfloat16)

    group = 8

    def step(g, carry):
        base = pl.multiple_of(g * (group * slot), 8)
        for i in range(group):
            r = g * group + i
            for j in range(slot):
                stage[pl.ds(base + i * slot + j, 1), :] = table[pl.ds(send_ref[j, r], 1), :]
        rows = pl.ds(base, group * slot)
        out_ref[rows, :] = stage[rows, :].astype(jnp.bfloat16)
        return carry

    lax.fori_loop(0, receivers // group, step, 0)


def send_rows_of(features, weight, send_rows, hub_rows):
    rows, width = features.shape[0], weight.shape[1]
    receivers, slot = send_rows.shape
    return pl.pallas_call(
        functools.partial(send_kernel, slot),
        out_shape=(
            jax.ShapeDtypeStruct((rows, width), jnp.bfloat16),
            jax.ShapeDtypeStruct((receivers * slot, width), jnp.bfloat16),
            jax.ShapeDtypeStruct((hub_rows.shape[0], width), jnp.bfloat16),
        ),
        in_specs=[SMEM, SMEM, VMEM, VMEM],
        out_specs=(VMEM, VMEM, VMEM),
        scratch_shapes=[
            pltpu.VMEM((rows, width), jnp.float32),
            pltpu.VMEM((receivers * slot, width), jnp.float32),
        ],
        compiler_params=pltpu.CompilerParams(vmem_limit_bytes=16 * MIB),
        cost_estimate=pl.CostEstimate(flops=2 * rows * width * width, bytes_accessed=2 * MIB, transcendentals=0),
        name="send_rows",
    )(send_rows.T, hub_rows, features, weight)


def near_kernel(rows_ref, blocks_ref, values_ref, mapped_ref, bias_ref, out_ref):
    tile = values_ref.shape[1]
    out_ref[...] = jnp.broadcast_to(bias_ref[...], out_ref.shape)

    def step(t, carry):
        rows = pl.ds(pl.multiple_of(rows_ref[t] * tile, tile), tile)
        block = pl.ds(pl.multiple_of(blocks_ref[t] * tile, tile), tile)
        out_ref[rows, :] += jnp.dot(values_ref[t], mapped_ref[block, :], preferred_element_type=jnp.float32)
        return carry

    lax.fori_loop(0, values_ref.shape[0], step, 0, unroll=4)


def near_part(rows_of, blocks_of, values, mapped, bias):
    tiles, tile = values.shape[:2]
    rows, width = mapped.shape
    return pl.pallas_call(
        near_kernel,
        out_shape=jax.ShapeDtypeStruct((rows, width), jnp.float32),
        in_specs=[SMEM, SMEM, VMEM, VMEM, VMEM],
        out_specs=VMEM,
        compiler_params=pltpu.CompilerParams(vmem_limit_bytes=16 * MIB),
        cost_estimate=pl.CostEstimate(
            flops=2 * tiles * tile * tile * width, bytes_accessed=4 * MIB, transcendentals=0
        ),
        name="near_part",
    )(rows_of, blocks_of, values, mapped, bias)


def hub_kernel(near_ref, weights_ref, hub_ref, out_ref, ordered):
    own = hub_ref.shape[0] // (Y * Z * CORES * X)

    def place(i, carry):
        z = i % Z
        y = i // Z
        for core in range(CORES):
            for x in range(X):
                src = pl.multiple_of((((core * X + x) * Y + y) * Z + z) * own, own)
                dst = pl.multiple_of((((y * Z + z) * CORES + core) * X + x) * own, own)
                ordered[pl.ds(dst, own), :] = hub_ref[pl.ds(src, own), :].astype(jnp.float32)
        return carry

    lax.fori_loop(0, Y * Z, place, 0)
    hub = ordered[...].astype(jnp.bfloat16)
    tile = 256

    def step(i, carry):
        rows = pl.ds(pl.multiple_of(i * tile, tile), tile)
        out_ref[rows, :] = near_ref[rows, :] + jnp.dot(
            weights_ref[rows, :], hub, preferred_element_type=jnp.float32
        )
        return carry

    lax.fori_loop(0, out_ref.shape[0] // tile, step, 0)


def add_hub_part(near, weights, hub):
    rows, width = near.shape
    return pl.pallas_call(
        hub_kernel,
        out_shape=jax.ShapeDtypeStruct((rows, width), jnp.float32),
        in_specs=[VMEM, VMEM, VMEM],
        out_specs=VMEM,
        scratch_shapes=[pltpu.VMEM(hub.shape, jnp.float32)],
        compiler_params=pltpu.CompilerParams(vmem_limit_bytes=16 * MIB),
        cost_estimate=pl.CostEstimate(
            flops=2 * rows * hub.shape[0] * width, bytes_accessed=6 * MIB, transcendentals=0
        ),
        name="hub_part",
    )(near, weights, hub)


def far_kernel(rows_ref, blocks_ref, values_ref, received_ref, near_ref, out_ref, total):
    tile = values_ref.shape[1]
    total[...] = near_ref[...]

    def step(t, carry):
        rows = pl.ds(pl.multiple_of(rows_ref[t] * tile, tile), tile)
        block = pl.ds(pl.multiple_of(blocks_ref[t] * tile, tile), tile)
        total[rows, :] += jnp.dot(values_ref[t], received_ref[block, :], preferred_element_type=jnp.float32)
        return carry

    lax.fori_loop(0, values_ref.shape[0], step, 0, unroll=4)
    out_ref[...] = jnp.maximum(total[...], 0.0).astype(out_ref.dtype)


def finish(rows_of, blocks_of, values, received, near):
    tiles, tile = values.shape[:2]
    rows, width = near.shape
    return pl.pallas_call(
        far_kernel,
        out_shape=jax.ShapeDtypeStruct((rows, width), jnp.bfloat16),
        in_specs=[SMEM, SMEM, VMEM, VMEM, VMEM],
        out_specs=VMEM,
        scratch_shapes=[pltpu.VMEM((rows, width), jnp.float32)],
        compiler_params=pltpu.CompilerParams(vmem_limit_bytes=16 * MIB),
        cost_estimate=pl.CostEstimate(
            flops=2 * tiles * tile * tile * width, bytes_accessed=5 * MIB, transcendentals=0
        ),
        name="far_part",
    )(rows_of, blocks_of, values, received, near)


def partner(axis_size, stride, span, step):
    return [(i, i + ((((i // stride) % span) ^ step) - ((i // stride) % span)) * stride) for i in range(axis_size)]


def gather_hub(hub_here):
    dom = lax.axis_index("dom")
    sub = lax.axis_index("sub")
    dom_count, sub_count = lax.axis_size("dom"), lax.axis_size("sub")
    z, y, core = (dom // CORES) % Z, dom // (CORES * Z), dom % CORES
    rounds = [("dom", dom_count, CORES, Z, step, z) for step in (1, 2, 4)]
    rounds += [("dom", dom_count, CORES * Z, Y, step, y) for step in (1, 2)]
    rounds += [("sub", sub_count, 1, X, step, sub) for step in (1, 2)]
    rounds += [("dom", dom_count, 1, CORES, 1, core)]
    held = hub_here
    for axis, count, stride, span, step, place in rounds:
        other = lax.ppermute(held, axis, partner(count, stride, span, step))
        upper = (place // step) % 2 == 1
        held = jnp.concatenate(
            [jnp.where(upper, other, held), jnp.where(upper, held, other)], axis=0
        )
    return held


def on_device(
    features,
    weight,
    layer_bias,
    local_rows,
    local_blocks,
    local_values,
    send_rows,
    bound_rows,
    bound_blocks,
    bound_values,
    hub_rows,
    hub_weights,
):
    width = weight.shape[1]
    mapped, boundary_out, hub_here = send_rows_of(features, weight, send_rows, hub_rows)
    arrived = lax.all_to_all(
        boundary_out.reshape(-1, 2, width), ("dom", "sub"), split_axis=0, concat_axis=0, tiled=True
    )
    received = arrived.reshape(-1, width)
    near = near_part(local_rows, local_blocks, local_values, mapped, layer_bias[None, :])
    near = add_hub_part(near, hub_weights, gather_hub(hub_here))
    return finish(bound_rows, bound_blocks, bound_values, received, near)


def solution(mesh):
    in_specs = (
        P(("dom", "sub"), None),
        P(),
        P(),
        P(("dom", "sub")),
        P(("dom", "sub")),
        P(("dom", "sub"), None, None),
        P(("dom", "sub"), None),
        P(("dom", "sub")),
        P(("dom", "sub")),
        P(("dom", "sub"), None, None),
        P(("dom", "sub")),
        P(("dom", "sub"), None),
    )
    out_specs = P(("dom", "sub"), None)
    return jax.shard_map(
        on_device, mesh=mesh, in_specs=in_specs, out_specs=out_specs, check_vma=False
    )
```

time: 259 us -> 85.7 us (0.33)
  blocking collectives: 130 us -> 0 us
  local copies, waits for them, and re-layouts: 48.8 us -> 7.06 us
  other arithmetic: 41 us -> 0.33 us
  starting transfers between devices: 17.5 us -> 41.6 us
  matrix products: 19.9 us -> 0 us
  Pallas kernels: 0 us -> 18.9 us
  waiting for transfers between devices: 0.01 us -> 17.4 us
    all_gather x1 -> x0, blocking collectives: 130 us -> none  [on_device(): lax.all_gather(hub_here, ('dom', 'sub'), axis=0, tiled=True)]
    scatter-add x2 -> x0, other arithmetic: 38.9 us -> none  [tile_sum(): jnp.zeros((row_tiles, tile_size, out_width), jnp.float32).at[rows_of]]
    ppermute x0 -> x8, starting transfers between devices: none -> 22.9 us  [gather_hub(): other = lax.ppermute(held, axis, partner(count, stride, span, step))]
    dot_general x4 -> x0, matrix products: 19.9 us -> none  [the longest x2 14.7 us: tile_sum(): jnp.einsum('tij,tjh->tih', values, blocks, preferred_element_type=jnp.flo...]
    pallas_call x0 -> x4, Pallas kernels: none -> 18.9 us  [the longest x1 5.79 us: finish(): pl.pallas_call(far_kernel, out_shape=jax.ShapeDtypeStruct((rows, width),...]
    gather x4 -> x0, local copies, waits for them, and re-layouts: 18.5 us -> none  [the longest x1 11.4 us: on_device(): mapped[send_rows.reshape(-1)]]
    dot_general x2 -> x0, local copies, waits for them, and re-layouts: 13.2 us -> none  [tile_sum(): jnp.einsum('tij,tjh->tih', values, blocks, preferred_element_type=jnp.flo...]
    ppermute x0 -> x8, waiting for transfers between devices: none -> 10.4 us  [gather_hub(): other = lax.ppermute(held, axis, partner(count, stride, span, step))]
  transfers between devices with their start and end apart: 2 -> 9, of which waited for: 0 -> 7; matrix products, arithmetic and copies ran while one was open for 14% -> 0% of each run, Pallas kernels for 0% -> 9%
where the time goes in v1:
time: 85.7 us; the launch traced here: 85.4 us
  starting transfers between devices  41.6 us (49%)
  Pallas kernels  18.9 us (22%)
  waiting for transfers between devices  17.4 us (20%)
  local copies, waits for them, and re-layouts  7.06 us (8%)
    ppermute x8, starting transfers between devices, gather_hub(): other = lax.ppermute(held, axis, partner(count, stride, span, step))  22.9 us
    all_to_all x1, starting transfers between devices, on_device(): lax.all_to_all(boundary_out.reshape(-1, 2, width), ('dom', 'sub'), split_...  18.7 us
    ppermute x8, waiting for transfers between devices, gather_hub(): other = lax.ppermute(held, axis, partner(count, stride, span, step))  10.4 us
    unnamed x24, local copies, waits for them, and re-layouts  7.06 us
    all_to_all x1, waiting for transfers between devices, on_device(): lax.all_to_all(boundary_out.reshape(-1, 2, width), ('dom', 'sub'), split_...  6.97 us
    pallas_call x1, Pallas kernels, finish(): pl.pallas_call(far_kernel, out_shape=jax.ShapeDtypeStruct((rows, width),...  5.79 us
    pallas_call x1, Pallas kernels, send_rows_of(): pl.pallas_call(functools.partial(send_kernel, slot), out_shape=(jax.Shape...  5.56 us
    pallas_call x1, Pallas kernels, near_part(): pl.pallas_call(near_kernel, out_shape=jax.ShapeDtypeStruct((rows, width),...  5.08 us
  transfers between devices with their start and end apart: 9, of which 7 were waited for; matrix products, arithmetic and copies ran while one was open for 0% of the time, Pallas kernels for 9%

profile of v1, /device:TPU:1, one launch (start us, length us, event | category | flops | bytes accessed | tf_op | source)
XLA Modules:
  0.0 85.4 jit_solution(13995551629267740764)
XLA Ops:
  0.0 1.0 %copy-done.3 = bf16[1024,128]{1,0:T(8,128)(2,1)S(1)} copy-done((bf16[1024,128]{1,0:T(8,128)(2,1)S(1)}, bf16[1024,128]{1,0:T(8,128)(2,1)}, u32[]{:S(2)}) %copy-start.3) | copy-done | bytes 262168
  1.0 0.8 copy-done.4
  1.8 0.7 copy-done.5
  2.5 0.7 copy-done.6
  3.1 5.6 %send_rows.1 = (bf16[1024,128]{1,0:T(8,128)(2,1)S(1)}, bf16[3072,128]{1,0:T(8,128)(2,1)}, bf16[8,128]{1,0:T(8,128)(2,1)S(1)}) custom-call(s32[12,256]{1,0:T(8,128)S(1)} %bitcast.5, s32[8]{0:T(128)S(1)} %copy-done.6, bf16[1024,128]{1,0:T(8,128)(2,1)S(1)} %copy-done.3, bf16[128,128]{1,0:T(8,128)(2,1)S(1)} %copy-done.4), custom_call_target="tpu_custom_call" | custom-call | flops 33554432 | bytes 2097152 | tf_op jit(solution)/shard_map/send_rows/pallas_call | solution.py:44
  8.7 2.5 %collective-permute-start = (bf16[8,128]{1,0:T(8,128)(2,1)S(1)}, bf16[8,128]{1,0:T(8,128)(2,1)S(1)}, u32[]{:S(2)}, u32[]{:S(2)}) collective-permute-start(bf16[8,128]{1,0:T(8,128)(2,1)S(1)} %get-tuple-element.10), channel_id=1, source_target_pairs={{0,8},{4,12},{8,0},{12,4},{16,24},{20,28},{24,16},{28,20},{32,40},... | collective-permute-start | bytes 6152 | tf_op jit(solution)/shard_map/ppermute | solution.py:181
  11.1 1.0 %collective-permute-done = bf16[8,128]{1,0:T(8,128)(2,1)S(1)} collective-permute-done((bf16[8,128]{1,0:T(8,128)(2,1)S(1)}, bf16[8,128]{1,0:T(8,128)(2,1)S(1)}, u32[]{:S(2)}, u32[]{:S(2)}) %collective-permute-start) | collective-permute-done | bytes 2080 | tf_op jit(solution)/shard_map/ppermute | solution.py:181
  12.1 3.1 %collective-permute-start.1 = (bf16[16,128]{1,0:T(8,128)(2,1)S(1)}, bf16[16,128]{1,0:T(8,128)(2,1)S(1)}, u32[]{:S(2)}, u32[]{:S(2)}) collective-permute-start(bf16[16,128]{1,0:T(8,128)(2,1)S(1)} %pad_maximum_fusion.7), channel_id=1, source_target_pairs={{0,16},{4,20},{8,24},{12,28},{16,0},{20,4},{24,8},{28,12},{32,48},... | collective-permute-start | bytes 12296 | tf_op jit(solution)/shard_map/ppermute | solution.py:181
  15.2 1.0 %collective-permute-done.1 = bf16[16,128]{1,0:T(8,128)(2,1)S(1)} collective-permute-done((bf16[16,128]{1,0:T(8,128)(2,1)S(1)}, bf16[16,128]{1,0:T(8,128)(2,1)S(1)}, u32[]{:S(2)}, u32[]{:S(2)}) %collective-permute-start.1) | collective-permute-done | bytes 4128 | tf_op jit(solution)/shard_map/ppermute | solution.py:181
  16.2 6.2 %collective-permute-start.2 = (bf16[32,128]{1,0:T(8,128)(2,1)S(1)}, bf16[32,128]{1,0:T(8,128)(2,1)S(1)}, u32[]{:S(2)}, u32[]{:S(2)}) collective-permute-start(bf16[32,128]{1,0:T(8,128)(2,1)S(1)} %pad_maximum_fusion.6), channel_id=1, source_target_pairs={{0,32},{4,36},{8,40},{12,44},{16,48},{20,52},{24,56},{28,60},{32,0... | collective-permute-start | bytes 24584 | tf_op jit(solution)/shard_map/ppermute | solution.py:181
  22.4 1.1 %collective-permute-done.2 = bf16[32,128]{1,0:T(8,128)(2,1)S(1)} collective-permute-done((bf16[32,128]{1,0:T(8,128)(2,1)S(1)}, bf16[32,128]{1,0:T(8,128)(2,1)S(1)}, u32[]{:S(2)}, u32[]{:S(2)}) %collective-permute-start.2) | collective-permute-done | bytes 8224 | tf_op jit(solution)/shard_map/ppermute | solution.py:181
  23.5 1.4 %collective-permute-start.3 = (bf16[64,128]{1,0:T(8,128)(2,1)S(1)}, bf16[64,128]{1,0:T(8,128)(2,1)S(1)}, u32[]{:S(2)}, u32[]{:S(2)}) collective-permute-start(bf16[64,128]{1,0:T(8,128)(2,1)S(1)} %pad_maximum_fusion.5), channel_id=1, source_target_pairs={{0,64},{4,68},{8,72},{12,76},{16,80},{20,84},{24,88},{28,92},{32,9... | collective-permute-start | bytes 49160 | tf_op jit(solution)/shard_map/ppermute | solution.py:181
  24.9 1.6 %collective-permute-done.3 = bf16[64,128]{1,0:T(8,128)(2,1)S(1)} collective-permute-done((bf16[64,128]{1,0:T(8,128)(2,1)S(1)}, bf16[64,128]{1,0:T(8,128)(2,1)S(1)}, u32[]{:S(2)}, u32[]{:S(2)}) %collective-permute-start.3) | collective-permute-done | bytes 16416 | tf_op jit(solution)/shard_map/ppermute | solution.py:181
  26.5 3.0 %collective-permute-start.4 = (bf16[128,128]{1,0:T(8,128)(2,1)S(1)}, bf16[128,128]{1,0:T(8,128)(2,1)S(1)}, u32[]{:S(2)}, u32[]{:S(2)}) collective-permute-start(bf16[128,128]{1,0:T(8,128)(2,1)S(1)} %pad_maximum_fusion.4), channel_id=1, source_target_pairs={{0,128},{4,132},{8,136},{12,140},{16,144},{20,148},{24,152},{28,15... | collective-permute-start | bytes 98312 | tf_op jit(solution)/shard_map/ppermute | solution.py:181
  29.5 1.4 %collective-permute-done.4 = bf16[128,128]{1,0:T(8,128)(2,1)S(1)} collective-permute-done((bf16[128,128]{1,0:T(8,128)(2,1)S(1)}, bf16[128,128]{1,0:T(8,128)(2,1)S(1)}, u32[]{:S(2)}, u32[]{:S(2)}) %collective-permute-start.4) | collective-permute-done | bytes 32800 | tf_op jit(solution)/shard_map/ppermute | solution.py:181
  30.9 1.3 %collective-permute-start.5 = (bf16[256,128]{1,0:T(8,128)(2,1)S(1)}, bf16[256,128]{1,0:T(8,128)(2,1)S(1)}, u32[]{:S(2)}, u32[]{:S(2)}) collective-permute-start(bf16[256,128]{1,0:T(8,128)(2,1)S(1)} %pad_maximum_fusion.3), channel_id=1, source_target_pairs={{0,1},{1,0},{2,3},{3,2},{4,5},{5,4},{6,7},{7,6},{8,9},{9,8},{10,11... | collective-permute-start | bytes 196616 | tf_op jit(solution)/shard_map/ppermute | solution.py:181
  32.2 18.7 %all-to-all-start = ((bf16[1536,2,128]{2,1,0:T(2,128)(2,1)}), bf16[1536,2,128]{2,1,0:T(2,128)(2,1)S(1)}, u32[]{:S(2)}, u32[]{:S(2)}) async-start(bf16[1536,2,128]{2,1,0:T(2,128)(2,1)} %bitcast.1), calls=%async_computation | async-start | bytes 1572864 | tf_op jit(solution)/shard_map/all_to_all | solution.py:205
  51.0 3.0 %collective-permute-start.6 = (bf16[512,128]{1,0:T(8,128)(2,1)S(1)}, bf16[512,128]{1,0:T(8,128)(2,1)S(1)}, u32[]{:S(2)}, u32[]{:S(2)}) collective-permute-start(bf16[512,128]{1,0:T(8,128)(2,1)S(1)} %pad_maximum_fusion.2), channel_id=1, source_target_pairs={{0,2},{1,3},{2,0},{3,1},{4,6},{5,7},{6,4},{7,5},{8,10},{9,11},{10,... | collective-permute-start | bytes 393224 | tf_op jit(solution)/shard_map/ppermute | solution.py:181
  53.9 4.4 %collective-permute-done.6 = bf16[512,128]{1,0:T(8,128)(2,1)S(1)} collective-permute-done((bf16[512,128]{1,0:T(8,128)(2,1)S(1)}, bf16[512,128]{1,0:T(8,128)(2,1)S(1)}, u32[]{:S(2)}, u32[]{:S(2)}) %collective-permute-start.6) | collective-permute-done | bytes 131104 | tf_op jit(solution)/shard_map/ppermute | solution.py:181
  58.3 0.1 broadcast_select_fusion.3
  58.4 2.5 %collective-permute-start.7 = (bf16[1024,128]{1,0:T(8,128)(2,1)S(1)}, bf16[1024,128]{1,0:T(8,128)(2,1)S(1)}, u32[]{:S(2)}, u32[]{:S(2)}) collective-permute-start(bf16[1024,128]{1,0:T(8,128)(2,1)S(1)} %pad_maximum_fusion.1), channel_id=1, source_target_pairs={{0,4},{4,0},{8,12},{12,8},{16,20},{20,16},{24,28},{28,24},{32,36},... | collective-permute-start | bytes 786440 | tf_op jit(solution)/shard_map/ppermute | solution.py:181
  61.0 0.0 copy-start.1
  61.0 2.0 %copy-done.1 = bf16[96,128,128]{2,1,0:T(8,128)(2,1)S(1)} copy-done((bf16[96,128,128]{2,1,0:T(8,128)(2,1)S(1)}, bf16[96,128,128]{2,1,0:T(8,128)(2,1)}, u32[]{:S(2)}) %copy-start.1) | copy-done | bytes 3145752
  63.0 5.1 %near_part.1.near_ref = f32[1024,128]{1,0:T(8,128)S(1)} custom-call(s32[96]{0:T(128)S(1)} %copy-done.7, s32[96]{0:T(128)S(1)} %copy-done.8, bf16[96,128,128]{2,1,0:T(8,128)(2,1)S(1)} %copy-done.1, bf16[1024,128]{1,0:T(8,128)(2,1)S(1)} %get-tuple-element.9.mapped_ref, f32[1,128]{1,0:T(1,128)S(1)} %bitcast.6), custom_call_target="tpu_custom_call" | custom-call | flops 402653184 | bytes 4194304 | tf_op jit(solution)/shard_map/near_part/pallas_call | solution.py:79
  68.1 0.0 collective-permute-done.7
  68.1 0.1 broadcast_select_fusion.1
  68.3 0.0 copy-start.10
  68.3 0.0 copy-start.11
  68.3 2.5 %hub_part.1.near_ref = f32[1024,128]{1,0:T(8,128)S(1)} custom-call(f32[1024,128]{1,0:T(8,128)S(1)} %near_part.1.near_ref, bf16[1024,2048]{1,0:T(8,128)(2,1)S(1)} %copy-done, bf16[2048,128]{1,0:T(8,128)(2,1)S(1)} %pad_maximum_fusion.hub_ref), custom_call_target="tpu_custom_call" | custom-call | flops 536870912 | bytes 6291456 | tf_op jit(solution)/shard_map/hub_part/pallas_call | solution.py:121
  70.8 7.0 %all-to-all-done = bf16[1536,2,128]{2,1,0:T(2,128)(2,1)S(1)} async-done(((bf16[1536,2,128]{2,1,0:T(2,128)(2,1)}), bf16[1536,2,128]{2,1,0:T(2,128)(2,1)S(1)}, u32[]{:S(2)}, u32[]{:S(2)}) %all-to-all-start) | async-done | bytes 786464 | tf_op jit(solution)/shard_map/all_to_all | solution.py:205
  77.8 1.9 %copy-done.2 = bf16[96,128,128]{2,1,0:T(8,128)(2,1)S(1)} copy-done((bf16[96,128,128]{2,1,0:T(8,128)(2,1)S(1)}, bf16[96,128,128]{2,1,0:T(8,128)(2,1)}, u32[]{:S(2)}) %copy-start.2) | copy-done | bytes 3145752
  79.6 5.8 %far_part.1 = bf16[1024,128]{1,0:T(8,128)(2,1)} custom-call(s32[96]{0:T(128)S(1)} %copy-done.10, s32[96]{0:T(128)S(1)} %copy-done.11, bf16[96,128,128]{2,1,0:T(8,128)(2,1)S(1)} %copy-done.2, bf16[3072,128]{1,0:T(8,128)(2,1)S(1)} %bitcast.4, f32[1024,128]{1,0:T(8,128)S(1)} %hub_part.1.near_ref), custom_call_target="tpu_custom_call" | custom-call | flops 402653184 | bytes 5242880 | tf_op jit(solution)/shard_map/far_part/pallas_call | solution.py:152
  (30 shorter events, 0.2 us)
Async XLA Ops:
  0.0 61.0 %copy-start.8 = (s32[96]{0:T(128)S(1)}, s32[96]{0:T(128)}, u32[]{:S(2)}) copy-start(s32[96]{0:T(128)} %blocks_ref.2) | copy-start | bytes 1156
  0.0 61.0 %copy-start.7 = (s32[96]{0:T(128)S(1)}, s32[96]{0:T(128)}, u32[]{:S(2)}) copy-start(s32[96]{0:T(128)} %rows_ref.2) | copy-start | bytes 1156
  0.0 61.0 %copy-start.9 = (f32[128]{0:T(128)S(1)}, f32[128]{0:T(128)}, u32[]{:S(2)}) copy-start(f32[128]{0:T(128)} %param.14) | copy-start | bytes 1540
  0.0 1.0 %copy-start.3 = (bf16[1024,128]{1,0:T(8,128)(2,1)S(1)}, bf16[1024,128]{1,0:T(8,128)(2,1)}, u32[]{:S(2)}) copy-start(bf16[1024,128]{1,0:T(8,128)(2,1)} %feat_ref.1) | copy-start | bytes 786436
  1.0 0.8 copy-start.4
  1.8 0.7 copy-start.5
  2.5 0.7 copy-start.6
  8.7 3.4 %collective-permute-start = (bf16[8,128]{1,0:T(8,128)(2,1)S(1)}, bf16[8,128]{1,0:T(8,128)(2,1)S(1)}, u32[]{:S(2)}, u32[]{:S(2)}) collective-permute-start(bf16[8,128]{1,0:T(8,128)(2,1)S(1)} %get-tuple-element.10), channel_id=1, source_target_pairs={{0,8},{4,12},{8,0},{12,4},{16,24},{20,28},{24,16},{28,20},{32,40},... | collective-permute-start | bytes 6152 | tf_op jit(solution)/shard_map/ppermute | solution.py:181
  12.1 4.1 %collective-permute-start.1 = (bf16[16,128]{1,0:T(8,128)(2,1)S(1)}, bf16[16,128]{1,0:T(8,128)(2,1)S(1)}, u32[]{:S(2)}, u32[]{:S(2)}) collective-permute-start(bf16[16,128]{1,0:T(8,128)(2,1)S(1)} %pad_maximum_fusion.7), channel_id=1, source_target_pairs={{0,16},{4,20},{8,24},{12,28},{16,0},{20,4},{24,8},{28,12},{32,48},... | collective-permute-start | bytes 12296 | tf_op jit(solution)/shard_map/ppermute | solution.py:181
  16.2 7.3 %collective-permute-start.2 = (bf16[32,128]{1,0:T(8,128)(2,1)S(1)}, bf16[32,128]{1,0:T(8,128)(2,1)S(1)}, u32[]{:S(2)}, u32[]{:S(2)}) collective-permute-start(bf16[32,128]{1,0:T(8,128)(2,1)S(1)} %pad_maximum_fusion.6), channel_id=1, source_target_pairs={{0,32},{4,36},{8,40},{12,44},{16,48},{20,52},{24,56},{28,60},{32,0... | collective-permute-start | bytes 24584 | tf_op jit(solution)/shard_map/ppermute | solution.py:181
  23.5 3.0 %collective-permute-start.3 = (bf16[64,128]{1,0:T(8,128)(2,1)S(1)}, bf16[64,128]{1,0:T(8,128)(2,1)S(1)}, u32[]{:S(2)}, u32[]{:S(2)}) collective-permute-start(bf16[64,128]{1,0:T(8,128)(2,1)S(1)} %pad_maximum_fusion.5), channel_id=1, source_target_pairs={{0,64},{4,68},{8,72},{12,76},{16,80},{20,84},{24,88},{28,92},{32,9... | collective-permute-start | bytes 49160 | tf_op jit(solution)/shard_map/ppermute | solution.py:181
  26.5 4.4 %collective-permute-start.4 = (bf16[128,128]{1,0:T(8,128)(2,1)S(1)}, bf16[128,128]{1,0:T(8,128)(2,1)S(1)}, u32[]{:S(2)}, u32[]{:S(2)}) collective-permute-start(bf16[128,128]{1,0:T(8,128)(2,1)S(1)} %pad_maximum_fusion.4), channel_id=1, source_target_pairs={{0,128},{4,132},{8,136},{12,140},{16,144},{20,148},{24,152},{28,15... | collective-permute-start | bytes 98312 | tf_op jit(solution)/shard_map/ppermute | solution.py:181
  30.9 20.0 %collective-permute-start.5 = (bf16[256,128]{1,0:T(8,128)(2,1)S(1)}, bf16[256,128]{1,0:T(8,128)(2,1)S(1)}, u32[]{:S(2)}, u32[]{:S(2)}) collective-permute-start(bf16[256,128]{1,0:T(8,128)(2,1)S(1)} %pad_maximum_fusion.3), channel_id=1, source_target_pairs={{0,1},{1,0},{2,3},{3,2},{4,5},{5,4},{6,7},{7,6},{8,9},{9,8},{10,11... | collective-permute-start | bytes 196616 | tf_op jit(solution)/shard_map/ppermute | solution.py:181
  32.2 45.5 %all-to-all-start = ((bf16[1536,2,128]{2,1,0:T(2,128)(2,1)}), bf16[1536,2,128]{2,1,0:T(2,128)(2,1)S(1)}, u32[]{:S(2)}, u32[]{:S(2)}) async-start(bf16[1536,2,128]{2,1,0:T(2,128)(2,1)} %bitcast.1), calls=%async_computation | async-start | bytes 1572864 | tf_op jit(solution)/shard_map/all_to_all | solution.py:205
  51.0 7.4 %collective-permute-start.6 = (bf16[512,128]{1,0:T(8,128)(2,1)S(1)}, bf16[512,128]{1,0:T(8,128)(2,1)S(1)}, u32[]{:S(2)}, u32[]{:S(2)}) collective-permute-start(bf16[512,128]{1,0:T(8,128)(2,1)S(1)} %pad_maximum_fusion.2), channel_id=1, source_target_pairs={{0,2},{1,3},{2,0},{3,1},{4,6},{5,7},{6,4},{7,5},{8,10},{9,11},{10,... | collective-permute-start | bytes 393224 | tf_op jit(solution)/shard_map/ppermute | solution.py:181
  58.4 9.7 %collective-permute-start.7 = (bf16[1024,128]{1,0:T(8,128)(2,1)S(1)}, bf16[1024,128]{1,0:T(8,128)(2,1)S(1)}, u32[]{:S(2)}, u32[]{:S(2)}) collective-permute-start(bf16[1024,128]{1,0:T(8,128)(2,1)S(1)} %pad_maximum_fusion.1), channel_id=1, source_target_pairs={{0,4},{4,0},{8,12},{12,8},{16,20},{20,16},{24,28},{28,24},{32,36},... | collective-permute-start | bytes 786440 | tf_op jit(solution)/shard_map/ppermute | solution.py:181
  61.0 7.3 %copy-start = (bf16[1024,2048]{1,0:T(8,128)(2,1)S(1)}, bf16[1024,2048]{1,0:T(8,128)(2,1)}, u32[]{:S(2)}) copy-start(bf16[1024,2048]{1,0:T(8,128)(2,1)} %weights_ref.1) | copy-start | bytes 12582916
  61.0 2.0 %copy-start.1 = (bf16[96,128,128]{2,1,0:T(8,128)(2,1)S(1)}, bf16[96,128,128]{2,1,0:T(8,128)(2,1)}, u32[]{:S(2)}) copy-start(bf16[96,128,128]{2,1,0:T(8,128)(2,1)} %values_ref.2) | copy-start | bytes 9437188
  68.3 9.5 %copy-start.10 = (s32[96]{0:T(128)S(1)}, s32[96]{0:T(128)}, u32[]{:S(2)}) copy-start(s32[96]{0:T(128)} %rows_ref.3) | copy-start | bytes 1156
  68.3 9.4 %copy-start.11 = (s32[96]{0:T(128)S(1)}, s32[96]{0:T(128)}, u32[]{:S(2)}) copy-start(s32[96]{0:T(128)} %blocks_ref.3) | copy-start | bytes 1156
  77.7 1.9 %copy-start.2 = (bf16[96,128,128]{2,1,0:T(8,128)(2,1)S(1)}, bf16[96,128,128]{2,1,0:T(8,128)(2,1)}, u32[]{:S(2)}) copy-start(bf16[96,128,128]{2,1,0:T(8,128)(2,1)} %values_ref.3) | copy-start | bytes 9437188

commit v2 on v1

v2 whole, which is shorter than its diff:
```python
import functools

import jax
import jax.numpy as jnp
from jax import lax
from jax.experimental import pallas as pl
from jax.experimental.pallas import tpu as pltpu
from jax.sharding import PartitionSpec as P

VMEM = pl.BlockSpec(memory_space=pltpu.VMEM)
SMEM = pl.BlockSpec(memory_space=pltpu.SMEM)
MIB = 1024 * 1024
Y, Z, CORES, X = 4, 8, 2, 4


def send_kernel(
    core_ref, own_ref, other_ref, hub_ref, feat_ref, near_feat_ref, weight_ref, mapped_ref, out_ref, table, near_table, stage
):
    slot = own_ref.shape[0]
    hubs = hub_ref.shape[0]
    message = 2 * slot + hubs
    core = core_ref[0]
    mapped = jnp.dot(feat_ref[...], weight_ref[...], preferred_element_type=jnp.float32)
    mapped = mapped.astype(jnp.bfloat16)
    mapped_ref[...] = mapped
    table[...] = mapped.astype(jnp.float32)
    far = jnp.dot(near_feat_ref[...], weight_ref[...], preferred_element_type=jnp.float32)
    near_table[...] = far.astype(jnp.bfloat16).astype(jnp.float32)
    hub_rows = jnp.concatenate([table[pl.ds(hub_ref[j], 1), :] for j in range(hubs)], axis=0)

    def step(g, carry):
        base = pl.multiple_of(g * (X * message), X * message)
        for x in range(X):
            r = (g * CORES + core) * X + x
            for j in range(slot):
                stage[pl.ds(base + x * message + j, 1), :] = table[pl.ds(own_ref[j, r], 1), :]
            for j in range(slot):
                stage[pl.ds(base + x * message + slot + j, 1), :] = near_table[pl.ds(other_ref[j, r], 1), :]
            stage[pl.ds(base + x * message + 2 * slot, hubs), :] = hub_rows
        rows = pl.ds(base, X * message)
        out_ref[rows, :] = stage[rows, :].astype(jnp.bfloat16)
        return carry

    lax.fori_loop(0, Y * Z, step, 0)


def messages_of(core, send_own, send_other, hub_rows, features, near_features, weight):
    rows, width = features.shape[0], weight.shape[1]
    slot, hubs = send_own.shape[0], hub_rows.shape[0]
    total = Y * Z * X * (2 * slot + hubs)
    return pl.pallas_call(
        send_kernel,
        out_shape=(
            jax.ShapeDtypeStruct((rows, width), jnp.bfloat16),
            jax.ShapeDtypeStruct((total, width), jnp.bfloat16),
        ),
        in_specs=[SMEM, SMEM, SMEM, SMEM, VMEM, VMEM, VMEM],
        out_specs=(VMEM, VMEM),
        scratch_shapes=[
            pltpu.VMEM((rows, width), jnp.float32),
            pltpu.VMEM((rows, width), jnp.float32),
            pltpu.VMEM((total, width), jnp.float32),
        ],
        compiler_params=pltpu.CompilerParams(vmem_limit_bytes=16 * MIB),
        cost_estimate=pl.CostEstimate(flops=4 * rows * width * width, bytes_accessed=2 * MIB, transcendentals=0),
        name="messages",
    )(core, send_own, send_other, hub_rows, features, near_features, weight)


def near_kernel(rows_ref, blocks_ref, values_ref, mapped_ref, bias_ref, out_ref):
    tile = values_ref.shape[1]
    out_ref[...] = jnp.broadcast_to(bias_ref[...], out_ref.shape)

    def step(t, carry):
        rows = pl.ds(pl.multiple_of(rows_ref[t] * tile, tile), tile)
        block = pl.ds(pl.multiple_of(blocks_ref[t] * tile, tile), tile)
        out_ref[rows, :] += jnp.dot(values_ref[t], mapped_ref[block, :], preferred_element_type=jnp.float32)
        return carry

    lax.fori_loop(0, values_ref.shape[0], step, 0, unroll=4)


def near_part(rows_of, blocks_of, values, mapped, bias):
    tiles, tile = values.shape[:2]
    rows, width = mapped.shape
    return pl.pallas_call(
        near_kernel,
        out_shape=jax.ShapeDtypeStruct((rows, width), jnp.float32),
        in_specs=[SMEM, SMEM, VMEM, VMEM, VMEM],
        out_specs=VMEM,
        compiler_params=pltpu.CompilerParams(vmem_limit_bytes=16 * MIB),
        cost_estimate=pl.CostEstimate(
            flops=2 * tiles * tile * tile * width, bytes_accessed=4 * MIB, transcendentals=0
        ),
        name="near_part",
    )(rows_of, blocks_of, values, mapped, bias)


def order_kernel(slot, core_ref, arrived_ref, received_ref, hub_ref):
    message = arrived_ref.shape[0] // (Y * Z * X)
    hubs = message - 2 * slot
    size = X * message
    bound = CORES * X * slot
    core = core_ref[0]
    n = lax.broadcasted_iota(jnp.int32, (size, size), 0)
    source = lax.broadcasted_iota(jnp.int32, (size, size), 1)
    sender = (n >= X * slot).astype(jnp.int32)
    place = n - sender * (X * slot)
    x = sum((place >= k * slot).astype(jnp.int32) for k in range(1, X))
    second = jnp.where(sender == core, 0, slot)
    wanted = x * message + second + (place - x * slot)
    hub_place = n - bound
    hub_x = sum((hub_place >= k * hubs).astype(jnp.int32) for k in range(1, X))
    wanted = jnp.where(n >= bound, hub_x * message + 2 * slot + (hub_place - hub_x * hubs), wanted)
    order = jnp.where(wanted == source, 1.0, 0.0).astype(jnp.bfloat16)

    def step(g, carry):
        chunk = arrived_ref[pl.ds(pl.multiple_of(g * size, size), size), :]
        sorted_rows = jnp.dot(order, chunk, preferred_element_type=jnp.float32).astype(jnp.bfloat16)
        received_ref[pl.ds(pl.multiple_of(g * bound, bound), bound), :] = sorted_rows[:bound]
        hub_ref[pl.ds(pl.multiple_of(g * X * hubs, X * hubs), X * hubs), :] = sorted_rows[bound:]
        return carry

    lax.fori_loop(0, Y * Z, step, 0, unroll=4)


def order_rows(core, arrived, slot):
    total, width = arrived.shape
    groups = Y * Z
    bound = groups * CORES * X * slot
    hubs = total - bound
    return pl.pallas_call(
        functools.partial(order_kernel, slot),
        out_shape=(
            jax.ShapeDtypeStruct((bound, width), jnp.bfloat16),
            jax.ShapeDtypeStruct((hubs, width), jnp.bfloat16),
        ),
        in_specs=[SMEM, VMEM],
        out_specs=(VMEM, VMEM),
        compiler_params=pltpu.CompilerParams(vmem_limit_bytes=16 * MIB),
        cost_estimate=pl.CostEstimate(flops=256 * total * width, bytes_accessed=2 * MIB, transcendentals=0),
        name="order_rows",
    )(core, arrived)


def far_kernel(rows_ref, blocks_ref, values_ref, received_ref, near_ref, out_ref):
    tile = values_ref.shape[1]
    out_ref[...] = near_ref[...]

    def step(t, carry):
        rows = pl.ds(pl.multiple_of(rows_ref[t] * tile, tile), tile)
        block = pl.ds(pl.multiple_of(blocks_ref[t] * tile, tile), tile)
        out_ref[rows, :] += jnp.dot(values_ref[t], received_ref[block, :], preferred_element_type=jnp.float32)
        return carry

    lax.fori_loop(0, values_ref.shape[0], step, 0, unroll=4)


def add_far_part(rows_of, blocks_of, values, received, near):
    tiles, tile = values.shape[:2]
    rows, width = near.shape
    return pl.pallas_call(
        far_kernel,
        out_shape=jax.ShapeDtypeStruct((rows, width), jnp.float32),
        in_specs=[SMEM, SMEM, VMEM, VMEM, VMEM],
        out_specs=VMEM,
        compiler_params=pltpu.CompilerParams(vmem_limit_bytes=16 * MIB),
        cost_estimate=pl.CostEstimate(
            flops=2 * tiles * tile * tile * width, bytes_accessed=5 * MIB, transcendentals=0
        ),
        name="far_part",
    )(rows_of, blocks_of, values, received, near)


def hub_kernel(core_ref, sum_ref, weights_ref, own_ref, other_ref, out_ref, hub):
    groups = Y * Z
    half = own_ref.shape[0] // groups
    core = core_ref[0]

    def place(g, carry):
        rows = pl.ds(pl.multiple_of(g * half, half), half)
        own_at = pl.multiple_of((g * CORES + core) * half, half)
        other_at = pl.multiple_of((g * CORES + 1 - core) * half, half)
        hub[pl.ds(own_at, half), :] = own_ref[rows, :]
        hub[pl.ds(other_at, half), :] = other_ref[rows, :]
        return carry

    lax.fori_loop(0, groups, place, 0, unroll=4)
    tile = 256

    def step(i, carry):
        rows = pl.ds(pl.multiple_of(i * tile, tile), tile)
        total = sum_ref[rows, :] + jnp.dot(weights_ref[rows, :], hub[...], preferred_element_type=jnp.float32)
        out_ref[rows, :] = jnp.maximum(total, 0.0).astype(out_ref.dtype)
        return carry

    lax.fori_loop(0, out_ref.shape[0] // tile, step, 0)


def finish(core, total, weights, own_hub, other_hub):
    rows, width = total.shape
    hubs = weights.shape[1]
    return pl.pallas_call(
        hub_kernel,
        out_shape=jax.ShapeDtypeStruct((rows, width), jnp.bfloat16),
        in_specs=[SMEM, VMEM, VMEM, VMEM, VMEM],
        out_specs=VMEM,
        scratch_shapes=[pltpu.VMEM((hubs, width), jnp.bfloat16)],
        compiler_params=pltpu.CompilerParams(vmem_limit_bytes=16 * MIB),
        cost_estimate=pl.CostEstimate(flops=2 * rows * hubs * width, bytes_accessed=6 * MIB, transcendentals=0),
        name="hub_part",
    )(core, total, weights, own_hub, other_hub)


def on_device(
    features,
    weight,
    layer_bias,
    local_rows,
    local_blocks,
    local_values,
    send_rows,
    bound_rows,
    bound_blocks,
    bound_values,
    hub_rows,
    hub_weights,
):
    width = weight.shape[1]
    slot = send_rows.shape[1]
    dom_count, sub_count = lax.axis_size("dom"), lax.axis_size("sub")
    core = (lax.axis_index("dom") % CORES).astype(jnp.int32).reshape(1)
    other_core = [(i, i ^ 1) for i in range(dom_count)]
    same_core = [
        [i for i in range(dom_count * sub_count) if (i // sub_count) % CORES == c] for c in range(CORES)
    ]

    send_own = send_rows.T
    send_other = lax.ppermute(send_own, "dom", other_core)
    near_features = lax.ppermute(features, "dom", other_core)
    mapped, messages = messages_of(core, send_own, send_other, hub_rows, features, near_features, weight)
    arrived = lax.all_to_all(
        messages.reshape(len(same_core[0]), -1, width),
        ("dom", "sub"),
        split_axis=0,
        concat_axis=0,
        tiled=True,
        axis_index_groups=same_core,
    ).reshape(-1, width)
    near = near_part(local_rows, local_blocks, local_values, mapped, layer_bias[None, :])
    received, own_hub = order_rows(core, arrived, slot)
    other_hub = lax.ppermute(own_hub, "dom", other_core)
    total = add_far_part(bound_rows, bound_blocks, bound_values, received, near)
    return finish(core, total, hub_weights, own_hub, other_hub)


def solution(mesh):
    in_specs = (
        P(("dom", "sub"), None),
        P(),
        P(),
        P(("dom", "sub")),
        P(("dom", "sub")),
        P(("dom", "sub"), None, None),
        P(("dom", "sub"), None),
        P(("dom", "sub")),
        P(("dom", "sub")),
        P(("dom", "sub"), None, None),
        P(("dom", "sub")),
        P(("dom", "sub"), None),
    )
    out_specs = P(("dom", "sub"), None)
    return jax.shard_map(
        on_device, mesh=mesh, in_specs=in_specs, out_specs=out_specs, check_vma=False
    )
```

time: 85.7 us -> 71.5 us (0.83)
  blocking collectives: 0 us -> 41.3 us
  starting transfers between devices: 41.6 us -> 6.79 us
  waiting for transfers between devices: 17.4 us -> 1.4 us
  local copies, waits for them, and re-layouts: 7.06 us -> 3.12 us
    all_to_all x0 -> x1, blocking collectives: none -> 41.3 us  [on_device(): lax.all_to_all(messages.reshape(len(same_core[0]), -1, width), ('dom', 's...]
    all_to_all x1 -> x0, starting transfers between devices: 18.7 us -> none  [on_device(): lax.all_to_all(boundary_out.reshape(-1, 2, width), ('dom', 'sub'), split_...]
    ppermute x8 -> x3, starting transfers between devices: 22.9 us -> 6.79 us  [the longest x1 3.55 us: on_device(): other_hub = lax.ppermute(own_hub, 'dom', other_core)]
    ppermute x8 -> x3, waiting for transfers between devices: 10.4 us -> 1.4 us  [the longest x1 1.39 us: on_device(): send_other = lax.ppermute(send_own, 'dom', other_core)]
    all_to_all x1 -> x0, waiting for transfers between devices: 6.97 us -> none  [on_device(): lax.all_to_all(boundary_out.reshape(-1, 2, width), ('dom', 'sub'), split_...]
    unnamed x24, local copies, waits for them, and re-layouts: 7.06 us -> 3.12 us
    pallas_call x3 -> x4, Pallas kernels: 13.8 us -> 13.5 us  [the longest x1 5.06 us: add_far_part(): pl.pallas_call(far_kernel, out_shape=jax.ShapeDtypeStruct((rows, width),...]
  transfers between devices with their start and end apart: 9 -> 3, of which waited for: 7 -> 1; matrix products, arithmetic and copies ran while one was open for 0% -> 0% of each run, Pallas kernels for 9% -> 14%
where the time goes in v2:
time: 71.5 us; the launch traced here: 71.2 us
  blocking collectives  41.3 us (58%)
  Pallas kernels  18.6 us (26%)
  starting transfers between devices  6.79 us (9%)
  local copies, waits for them, and re-layouts  3.12 us (4%)
  waiting for transfers between devices  1.4 us (2%)
    all_to_all x1, blocking collectives, on_device(): lax.all_to_all(messages.reshape(len(same_core[0]), -1, width), ('dom', 's...  41.3 us
    pallas_call x1, Pallas kernels, add_far_part(): pl.pallas_call(far_kernel, out_shape=jax.ShapeDtypeStruct((rows, width),...  5.06 us
    pallas_call x1, Pallas kernels, near_part(): pl.pallas_call(near_kernel, out_shape=jax.ShapeDtypeStruct((rows, width),...  5.06 us
    pallas_call x1, Pallas kernels, messages_of(): pl.pallas_call(send_kernel, out_shape=(jax.ShapeDtypeStruct((rows, width)...  4.38 us
    ppermute x1, starting transfers between devices, on_device(): other_hub = lax.ppermute(own_hub, 'dom', other_core)  3.55 us
    ppermute x1, starting transfers between devices, on_device(): near_features = lax.ppermute(features, 'dom', other_core)  3.24 us
    unnamed x24, local copies, waits for them, and re-layouts  3.12 us
    pallas_call x1, Pallas kernels, finish(): pl.pallas_call(hub_kernel, out_shape=jax.ShapeDtypeStruct((rows, width),...  2.63 us
  transfers between devices with their start and end apart: 3, of which 1 were waited for; matrix products, arithmetic and copies ran while one was open for 0% of the time, Pallas kernels for 14%

profile of v2, /device:TPU:1, one launch (start us, length us, event | category | flops | bytes accessed | tf_op | source)
XLA Modules:
  0.0 71.2 jit_solution(3633419813571996634)
XLA Ops:
  0.0 0.0 copy-start.1
  0.0 3.2 %collective-permute-start.1 = (bf16[1024,128]{1,0:T(8,128)(2,1)}, bf16[1024,128]{1,0:T(8,128)(2,1)S(1)}, u32[]{:S(2)}, u32[]{:S(2)}) collective-permute-start(bf16[1024,128]{1,0:T(8,128)(2,1)} %feat_ref.1), channel_id=1, source_target_pairs={{0,4},{4,0},{8,12},{12,8},{16,20},{20,16},{24,28},{28,24},{32,36},... | collective-permute-start | bytes 786440 | tf_op jit(solution)/shard_map/ppermute | solution.py:240
  3.2 0.0 collective-permute-start
  3.2 1.4 %collective-permute-done.other_ref = s32[12,256]{1,0:T(8,128)S(1)} collective-permute-done((s32[12,256]{1,0:T(8,128)}, s32[12,256]{1,0:T(8,128)S(1)}, u32[]{:S(2)}, u32[]{:S(2)}) %collective-permute-start) | collective-permute-done | bytes 12320 | tf_op jit(solution)/shard_map/ppermute | solution.py:239
  4.6 0.0 collective-permute-done.1.near_feat_ref
  4.6 0.0 copy-start.3
  4.6 0.9 %copy-done.3 = bf16[1024,128]{1,0:T(8,128)(2,1)S(1)} copy-done((bf16[1024,128]{1,0:T(8,128)(2,1)S(1)}, bf16[1024,128]{1,0:T(8,128)(2,1)}, u32[]{:S(2)}) %copy-start.3) | copy-done | bytes 262168
  5.6 0.0 copy-start.4
  5.6 0.8 %copy-done.4 = bf16[128,128]{1,0:T(8,128)(2,1)S(1)} copy-done((bf16[128,128]{1,0:T(8,128)(2,1)S(1)}, bf16[128,128]{1,0:T(8,128)(2,1)}, u32[]{:S(2)}) %copy-start.4) | copy-done | bytes 32792
  6.4 0.0 copy-start.5
  6.4 0.7 %copy-done.5 = s32[256,12]{0,1:T(8,128)S(1)} copy-done((s32[256,12]{0,1:T(8,128)S(1)}, s32[256,12]{0,1:T(8,128)}, u32[]{:S(2)}) %copy-start.5) | copy-done | bytes 12312
  7.1 0.7 copy-done.6
  7.7 4.4 %messages.1 = (bf16[1024,128]{1,0:T(8,128)(2,1)S(1)}, bf16[4096,128]{1,0:T(8,128)(2,1)S(1)}) custom-call(s32[1]{0:T(128)} %bitcast.core_ref, s32[12,256]{1,0:T(8,128)S(1)} %bitcast.8, s32[12,256]{1,0:T(8,128)S(1)} %collective-permute-done.other_ref, s32[8]{0:T(128)S(1)} %copy-done.6, bf16[1024,128]{1,0:T(8,128)(2,1)S(1)} %copy-done.3, ...), custom_call_target="tpu_custom_call" | custom-call | flops 67108864 | bytes 2097152 | tf_op jit(solution)/shard_map/messages/pallas_call | solution.py:51
  12.1 0.0 copy-start.2
  12.1 0.0 copy-start.10
  12.1 0.0 copy-start.11
  12.1 41.3 %all_to_all.5 = bf16[128,32,128]{2,1,0:T(8,128)(2,1)S(1)} all-to-all(bf16[128,32,128]{2,1,0:T(8,128)(2,1)S(1)} %bitcast.6), channel_id=1, replica_groups={{0,1,2,3,8,9,10,11,16,17,18,19,24,25,26,27,32,33,34,35,40,41,42,43,48,4..., dimensions={0} | all-to-all | bytes 2097152 | tf_op jit(solution)/shard_map/all_to_all | solution.py:242
  53.4 1.4 %order_rows.1 = (bf16[3072,128]{1,0:T(8,128)(2,1)S(1)}, bf16[1024,128]{1,0:T(8,128)(2,1)S(1)}) custom-call(s32[1]{0:T(128)} %bitcast.core_ref, bf16[4096,128]{1,0:T(8,128)(2,1)S(1)} %bitcast.5), custom_call_target="tpu_custom_call" | custom-call | flops 134217728 | bytes 2097152 | tf_op jit(solution)/shard_map/order_rows/pallas_call | solution.py:132
  54.9 3.5 %collective-permute-start.2 = (bf16[1024,128]{1,0:T(8,128)(2,1)S(1)}, bf16[1024,128]{1,0:T(8,128)(2,1)S(1)}, u32[]{:S(2)}, u32[]{:S(2)}) collective-permute-start(bf16[1024,128]{1,0:T(8,128)(2,1)S(1)} %get-tuple-element.12.own_ref), channel_id=1, source_target_pairs={{0,4},{4,0},{8,12},{12,8},{16,20},{20,16},{24,28},{28,24},{32,36},... | collective-permute-start | bytes 786440 | tf_op jit(solution)/shard_map/ppermute | solution.py:252
  58.4 0.0 copy-done.1
  58.4 0.0 copy-done.7
  58.4 0.0 copy-done.8
  58.4 0.0 copy-done.9
  58.4 5.1 %near_part.1.near_ref = f32[1024,128]{1,0:T(8,128)S(1)} custom-call(s32[96]{0:T(128)S(1)} %copy-done.7, s32[96]{0:T(128)S(1)} %copy-done.8, bf16[96,128,128]{2,1,0:T(8,128)(2,1)S(1)} %copy-done.1, bf16[1024,128]{1,0:T(8,128)(2,1)S(1)} %get-tuple-element.11.mapped_ref, f32[1,128]{1,0:T(1,128)S(1)} %bitcast.9), custom_call_target="tpu_custom_call" | custom-call | flops 402653184 | bytes 4194304 | tf_op jit(solution)/shard_map/near_part/pallas_call | solution.py:86
  63.5 0.0 copy-start
  63.5 0.0 copy-done.2
  63.5 0.0 copy-done.10
  63.5 0.0 copy-done.11
  63.5 5.1 %far_part.1.sum_ref = f32[1024,128]{1,0:T(8,128)S(1)} custom-call(s32[96]{0:T(128)S(1)} %copy-done.10, s32[96]{0:T(128)S(1)} %copy-done.11, bf16[96,128,128]{2,1,0:T(8,128)(2,1)S(1)} %copy-done.2, bf16[3072,128]{1,0:T(8,128)(2,1)S(1)} %get-tuple-element.10.received_ref, f32[1024,128]{1,0:T(8,128)S(1)} %near_part.1.near_ref), custom_call_target="tpu_custom_call" | custom-call | flops 402653184 | bytes 5242880 | tf_op jit(solution)/shard_map/far_part/pallas_call | solution.py:162
  68.6 0.0 collective-permute-done.2.other_ref
  68.6 0.0 copy-done
  68.6 2.6 %hub_part.1 = bf16[1024,128]{1,0:T(8,128)(2,1)} custom-call(s32[1]{0:T(128)} %bitcast.core_ref, f32[1024,128]{1,0:T(8,128)S(1)} %far_part.1.sum_ref, bf16[1024,2048]{1,0:T(8,128)(2,1)S(1)} %copy-done, bf16[1024,128]{1,0:T(8,128)(2,1)S(1)} %get-tuple-element.12.own_ref, bf16[1024,128]{1,0:T(8,128)(2,1)S(1)} %collective-permute-done.2.other_ref), custom_call_target="tpu_custom_call" | custom-call | flops 536870912 | bytes 6291456 | tf_op jit(solution)/shard_map/hub_part/pallas_call | solution.py:203
  (4 shorter events, 0.0 us)
Async XLA Ops:
  0.0 58.4 %copy-start.1 = (bf16[96,128,128]{2,1,0:T(8,128)(2,1)S(1)}, bf16[96,128,128]{2,1,0:T(8,128)(2,1)}, u32[]{:S(2)}) copy-start(bf16[96,128,128]{2,1,0:T(8,128)(2,1)} %values_ref.2) | copy-start | bytes 9437188
  0.0 4.6 %collective-permute-start.1 = (bf16[1024,128]{1,0:T(8,128)(2,1)}, bf16[1024,128]{1,0:T(8,128)(2,1)S(1)}, u32[]{:S(2)}, u32[]{:S(2)}) collective-permute-start(bf16[1024,128]{1,0:T(8,128)(2,1)} %feat_ref.1), channel_id=1, source_target_pairs={{0,4},{4,0},{8,12},{12,8},{16,20},{20,16},{24,28},{28,24},{32,36},... | collective-permute-start | bytes 786440 | tf_op jit(solution)/shard_map/ppermute | solution.py:240
  3.2 1.4 %collective-permute-start = (s32[12,256]{1,0:T(8,128)}, s32[12,256]{1,0:T(8,128)S(1)}, u32[]{:S(2)}, u32[]{:S(2)}) collective-permute-start(s32[12,256]{1,0:T(8,128)} %bitcast.7), channel_id=1, source_target_pairs={{0,4},{4,0},{8,12},{12,8},{16,20},{20,16},{24,28},{28,24},{32,36},... | collective-permute-start | bytes 36872 | tf_op jit(solution)/shard_map/ppermute | solution.py:239
  4.6 1.0 %copy-start.3 = (bf16[1024,128]{1,0:T(8,128)(2,1)S(1)}, bf16[1024,128]{1,0:T(8,128)(2,1)}, u32[]{:S(2)}) copy-start(bf16[1024,128]{1,0:T(8,128)(2,1)} %feat_ref.1) | copy-start | bytes 786436
  5.6 0.8 %copy-start.4 = (bf16[128,128]{1,0:T(8,128)(2,1)S(1)}, bf16[128,128]{1,0:T(8,128)(2,1)}, u32[]{:S(2)}) copy-start(bf16[128,128]{1,0:T(8,128)(2,1)} %weight_ref.1) | copy-start | bytes 98308
  6.4 0.7 %copy-start.5 = (s32[256,12]{0,1:T(8,128)S(1)}, s32[256,12]{0,1:T(8,128)}, u32[]{:S(2)}) copy-start(s32[256,12]{0,1:T(8,128)} %param.18) | copy-start | bytes 36868
  7.1 0.7 copy-start.6
  7.7 50.7 %copy-start.7 = (s32[96]{0:T(128)S(1)}, s32[96]{0:T(128)}, u32[]{:S(2)}) copy-start(s32[96]{0:T(128)} %rows_ref.2) | copy-start | bytes 1156
  7.7 50.7 %copy-start.8 = (s32[96]{0:T(128)S(1)}, s32[96]{0:T(128)}, u32[]{:S(2)}) copy-start(s32[96]{0:T(128)} %blocks_ref.2) | copy-start | bytes 1156
  7.7 50.7 %copy-start.9 = (f32[128]{0:T(128)S(1)}, f32[128]{0:T(128)}, u32[]{:S(2)}) copy-start(f32[128]{0:T(128)} %param.14) | copy-start | bytes 1540
  12.1 51.4 %copy-start.2 = (bf16[96,128,128]{2,1,0:T(8,128)(2,1)S(1)}, bf16[96,128,128]{2,1,0:T(8,128)(2,1)}, u32[]{:S(2)}) copy-start(bf16[96,128,128]{2,1,0:T(8,128)(2,1)} %values_ref.3) | copy-start | bytes 9437188
  12.1 51.4 %copy-start.10 = (s32[96]{0:T(128)S(1)}, s32[96]{0:T(128)}, u32[]{:S(2)}) copy-start(s32[96]{0:T(128)} %rows_ref.3) | copy-start | bytes 1156
  12.1 51.4 %copy-start.11 = (s32[96]{0:T(128)S(1)}, s32[96]{0:T(128)}, u32[]{:S(2)}) copy-start(s32[96]{0:T(128)} %blocks_ref.3) | copy-start | bytes 1156
  54.9 13.7 %collective-permute-start.2 = (bf16[1024,128]{1,0:T(8,128)(2,1)S(1)}, bf16[1024,128]{1,0:T(8,128)(2,1)S(1)}, u32[]{:S(2)}, u32[]{:S(2)}) collective-permute-start(bf16[1024,128]{1,0:T(8,128)(2,1)S(1)} %get-tuple-element.12.own_ref), channel_id=1, source_target_pairs={{0,4},{4,0},{8,12},{12,8},{16,20},{20,16},{24,28},{28,24},{32,36},... | collective-permute-start | bytes 786440 | tf_op jit(solution)/shard_map/ppermute | solution.py:252
  63.5 5.1 %copy-start = (bf16[1024,2048]{1,0:T(8,128)(2,1)S(1)}, bf16[1024,2048]{1,0:T(8,128)(2,1)}, u32[]{:S(2)}) copy-start(bf16[1024,2048]{1,0:T(8,128)(2,1)} %weights_ref.1) | copy-start | bytes 12582916

commit v3 on v2

--- a/solution.py
+++ b/solution.py
@@ -14,34 +14,50 @@
 
 
 def send_kernel(
-    core_ref, own_ref, other_ref, hub_ref, feat_ref, near_feat_ref, weight_ref, mapped_ref, out_ref, table, near_table, stage
+    core_ref, own_hbm, other_hbm, hub_hbm, feat_hbm, near_feat_hbm, weight_hbm, mapped_ref, out_ref,
+    own, other, hub, feat, near_feat, weight, table, near_table, stage, sems
 ):
-    slot = own_ref.shape[0]
-    hubs = hub_ref.shape[0]
+    pairs = (
+        (feat_hbm, feat), (weight_hbm, weight), (near_feat_hbm, near_feat),
+        (own_hbm, own), (other_hbm, other), (hub_hbm, hub),
+    )
+    copies = [pltpu.make_async_copy(src, dst, sems.at[i]) for i, (src, dst) in enumerate(pairs)]
+    for copy in copies:
+        copy.start()
+    slot = own.shape[0]
+    hubs = hub.shape[0]
     message = 2 * slot + hubs
     core = core_ref[0]
-    mapped = jnp.dot(feat_ref[...], weight_ref[...], preferred_element_type=jnp.float32)
+    copies[0].wait()
+    copies[1].wait()
+    mapped = jnp.dot(feat[...], weight[...], preferred_element_type=jnp.float32)
     mapped = mapped.astype(jnp.bfloat16)
     mapped_ref[...] = mapped
     table[...] = mapped.astype(jnp.float32)
-    far = jnp.dot(near_feat_ref[...], weight_ref[...], preferred_element_type=jnp.float32)
+    copies[2].wait()
+    far = jnp.dot(near_feat[...], weight[...], preferred_element_type=jnp.float32)
     near_table[...] = far.astype(jnp.bfloat16).astype(jnp.float32)
-    hub_rows = jnp.concatenate([table[pl.ds(hub_ref[j], 1), :] for j in range(hubs)], axis=0)
+    for copy in copies[3:]:
+        copy.wait()
+    hub_rows = jnp.concatenate([table[pl.ds(hub[j], 1), :] for j in range(hubs)], axis=0)
 
     def step(g, carry):
         base = pl.multiple_of(g * (X * message), X * message)
         for x in range(X):
             r = (g * CORES + core) * X + x
             for j in range(slot):
-                stage[pl.ds(base + x * message + j, 1), :] = table[pl.ds(own_ref[j, r], 1), :]
+                stage[pl.ds(base + x * message + j, 1), :] = table[pl.ds(own[j, r], 1), :]
             for j in range(slot):
-                stage[pl.ds(base + x * message + slot + j, 1), :] = near_table[pl.ds(other_ref[j, r], 1), :]
+                stage[pl.ds(base + x * message + slot + j, 1), :] = near_table[pl.ds(other[j, r], 1), :]
             stage[pl.ds(base + x * message + 2 * slot, hubs), :] = hub_rows
         rows = pl.ds(base, X * message)
         out_ref[rows, :] = stage[rows, :].astype(jnp.bfloat16)
         return carry
 
     lax.fori_loop(0, Y * Z, step, 0)
+
+
+HBM = pl.BlockSpec(memory_space=pltpu.HBM)
 
 
 def messages_of(core, send_own, send_other, hub_rows, features, near_features, weight):
@@ -54,14 +70,21 @@
             jax.ShapeDtypeStruct((rows, width), jnp.bfloat16),
             jax.ShapeDtypeStruct((total, width), jnp.bfloat16),
         ),
-        in_specs=[SMEM, SMEM, SMEM, SMEM, VMEM, VMEM, VMEM],
+        in_specs=[SMEM, HBM, HBM, HBM, HBM, HBM, HBM],
         out_specs=(VMEM, VMEM),
         scratch_shapes=[
+            pltpu.SMEM(send_own.shape, jnp.int32),
+            pltpu.SMEM(send_own.shape, jnp.int32),
+            pltpu.SMEM(hub_rows.shape, jnp.int32),
+            pltpu.VMEM(features.shape, jnp.bfloat16),
+            pltpu.VMEM(features.shape, jnp.bfloat16),
+            pltpu.VMEM(weight.shape, jnp.bfloat16),
             pltpu.VMEM((rows, width), jnp.float32),
             pltpu.VMEM((rows, width), jnp.float32),
             pltpu.VMEM((total, width), jnp.float32),
+            pltpu.SemaphoreType.DMA((6,)),
         ],
-        compiler_params=pltpu.CompilerParams(vmem_limit_bytes=16 * MIB),
+        compiler_params=pltpu.CompilerParams(vmem_limit_bytes=56 * MIB),
         cost_estimate=pl.CostEstimate(flops=4 * rows * width * width, bytes_accessed=2 * MIB, transcendentals=0),
         name="messages",
     )(core, send_own, send_other, hub_rows, features, near_features, weight)
@@ -77,7 +100,7 @@
         out_ref[rows, :] += jnp.dot(values_ref[t], mapped_ref[block, :], preferred_element_type=jnp.float32)
         return carry
 
-    lax.fori_loop(0, values_ref.shape[0], step, 0, unroll=4)
+    lax.fori_loop(0, values_ref.shape[0], step, 0, unroll=32)
 
 
 def near_part(rows_of, blocks_of, values, mapped, bias):
@@ -96,7 +119,7 @@
     )(rows_of, blocks_of, values, mapped, bias)
 
 
-def order_kernel(slot, core_ref, arrived_ref, received_ref, hub_ref):
+def order_kernel(slot, core_ref, arrived_ref, after_ref, received_ref, hub_ref):
     message = arrived_ref.shape[0] // (Y * Z * X)
     hubs = message - 2 * slot
     size = X * message
@@ -121,10 +144,10 @@
         hub_ref[pl.ds(pl.multiple_of(g * X * hubs, X * hubs), X * hubs), :] = sorted_rows[bound:]
         return carry
 
-    lax.fori_loop(0, Y * Z, step, 0, unroll=4)
-
-
-def order_rows(core, arrived, slot):
+    lax.fori_loop(0, Y * Z, step, 0, unroll=16)
+
+
+def order_rows(core, arrived, slot, after):
     total, width = arrived.shape
     groups = Y * Z
     bound = groups * CORES * X * slot
@@ -135,12 +158,12 @@
             jax.ShapeDtypeStruct((bound, width), jnp.bfloat16),
             jax.ShapeDtypeStruct((hubs, width), jnp.bfloat16),
         ),
-        in_specs=[SMEM, VMEM],
+        in_specs=[SMEM, VMEM, pl.BlockSpec(memory_space=pl.ANY)],
         out_specs=(VMEM, VMEM),
         compiler_params=pltpu.CompilerParams(vmem_limit_bytes=16 * MIB),
         cost_estimate=pl.CostEstimate(flops=256 * total * width, bytes_accessed=2 * MIB, transcendentals=0),
         name="order_rows",
-    )(core, arrived)
+    )(core, arrived, after)
 
 
 def far_kernel(rows_ref, blocks_ref, values_ref, received_ref, near_ref, out_ref):
@@ -153,7 +176,7 @@
         out_ref[rows, :] += jnp.dot(values_ref[t], received_ref[block, :], preferred_element_type=jnp.float32)
         return carry
 
-    lax.fori_loop(0, values_ref.shape[0], step, 0, unroll=4)
+    lax.fori_loop(0, values_ref.shape[0], step, 0, unroll=32)
 
 
 def add_far_part(rows_of, blocks_of, values, received, near):
@@ -185,7 +208,7 @@
         hub[pl.ds(other_at, half), :] = other_ref[rows, :]
         return carry
 
-    lax.fori_loop(0, groups, place, 0, unroll=4)
+    lax.fori_loop(0, groups, place, 0, unroll=8)
     tile = 256
 
     def step(i, carry):
@@ -248,7 +271,7 @@
         axis_index_groups=same_core,
     ).reshape(-1, width)
     near = near_part(local_rows, local_blocks, local_values, mapped, layer_bias[None, :])
-    received, own_hub = order_rows(core, arrived, slot)
+    received, own_hub = order_rows(core, arrived, slot, near)
     other_hub = lax.ppermute(own_hub, "dom", other_core)
     total = add_far_part(bound_rows, bound_blocks, bound_values, received, near)
     return finish(core, total, hub_weights, own_hub, other_hub)

time: 71.5 us -> 63.3 us (0.89)
  blocking collectives: 41.3 us -> 0 us
  waiting for transfers between devices: 1.4 us -> 21.9 us
  starting transfers between devices: 6.79 us -> 20.6 us
  Pallas kernels: 18.6 us -> 13 us
  local copies, waits for them, and re-layouts: 3.12 us -> 7.42 us
    all_to_all x1 -> x0, blocking collectives: 41.3 us -> none  [on_device(): lax.all_to_all(messages.reshape(len(same_core[0]), -1, width), ('dom', 's...]
    all_to_all x0 -> x1, waiting for transfers between devices: none -> 20.5 us  [on_device(): lax.all_to_all(messages.reshape(len(same_core[0]), -1, width), ('dom', 's...]
    all_to_all x0 -> x1, starting transfers between devices: none -> 13.8 us  [on_device(): lax.all_to_all(messages.reshape(len(same_core[0]), -1, width), ('dom', 's...]
    unnamed x24 -> x22, local copies, waits for them, and re-layouts: 3.12 us -> 7.42 us
    pallas_call x1, Pallas kernels: 5.06 us -> 2.01 us  [add_far_part(): pl.pallas_call(far_kernel, out_shape=jax.ShapeDtypeStruct((rows, width),...]
    pallas_call x1, Pallas kernels: 5.06 us -> 2.04 us  [near_part(): pl.pallas_call(near_kernel, out_shape=jax.ShapeDtypeStruct((rows, width),...]
    pallas_call x1, Pallas kernels: 4.38 us -> 5.72 us  [messages_of(): pl.pallas_call(send_kernel, out_shape=(jax.ShapeDtypeStruct((rows, width)...]
    pallas_call x1, Pallas kernels: 1.44 us -> 0.6 us  [order_rows(): pl.pallas_call(functools.partial(order_kernel, slot), out_shape=(jax.Shap...]
  transfers between devices with their start and end apart: 3 -> 4, of which waited for: 1 -> 2; matrix products, arithmetic and copies ran while one was open for 0% -> 0% of each run, Pallas kernels for 14% -> 6%
where the time goes in v3:
time: 63.3 us; the launch traced here: 63 us
  waiting for transfers between devices  21.9 us (35%)
  starting transfers between devices  20.6 us (33%)
  Pallas kernels  13 us (21%)
  local copies, waits for them, and re-layouts  7.42 us (12%)
    all_to_all x1, waiting for transfers between devices, on_device(): lax.all_to_all(messages.reshape(len(same_core[0]), -1, width), ('dom', 's...  20.5 us
    all_to_all x1, starting transfers between devices, on_device(): lax.all_to_all(messages.reshape(len(same_core[0]), -1, width), ('dom', 's...  13.8 us
    unnamed x22, local copies, waits for them, and re-layouts  7.42 us
    pallas_call x1, Pallas kernels, messages_of(): pl.pallas_call(send_kernel, out_shape=(jax.ShapeDtypeStruct((rows, width)...  5.72 us
    ppermute x1, starting transfers between devices, on_device(): other_hub = lax.ppermute(own_hub, 'dom', other_core)  3.55 us
    ppermute x1, starting transfers between devices, on_device(): near_features = lax.ppermute(features, 'dom', other_core)  3.24 us
    pallas_call x1, Pallas kernels, finish(): pl.pallas_call(hub_kernel, out_shape=jax.ShapeDtypeStruct((rows, width),...  2.62 us
    pallas_call x1, Pallas kernels, near_part(): pl.pallas_call(near_kernel, out_shape=jax.ShapeDtypeStruct((rows, width),...  2.04 us
  transfers between devices with their start and end apart: 4, of which 2 were waited for; matrix products, arithmetic and copies ran while one was open for 0% of the time, Pallas kernels for 6%

profile of v3, /device:TPU:1, one launch (start us, length us, event | category | flops | bytes accessed | tf_op | source)
XLA Modules:
  0.0 63.0 jit_solution(5210120914409454364)
XLA Ops:
  0.0 3.2 %collective-permute-start.1 = (bf16[1024,128]{1,0:T(8,128)(2,1)}, bf16[1024,128]{1,0:T(8,128)(2,1)S(1)}, u32[]{:S(2)}, u32[]{:S(2)}) collective-permute-start(bf16[1024,128]{1,0:T(8,128)(2,1)} %feat_hbm.1), channel_id=1, source_target_pairs={{0,4},{4,0},{8,12},{12,8},{16,20},{20,16},{24,28},{28,24},{32,36},... | collective-permute-start | bytes 786440 | tf_op jit(solution)/shard_map/ppermute | solution.py:263
  3.2 0.0 collective-permute-start
  3.2 1.4 %collective-permute-done.other_hbm = s32[12,256]{1,0:T(8,128)S(1)} collective-permute-done((s32[12,256]{1,0:T(8,128)}, s32[12,256]{1,0:T(8,128)S(1)}, u32[]{:S(2)}, u32[]{:S(2)}) %collective-permute-start) | collective-permute-done | bytes 12320 | tf_op jit(solution)/shard_map/ppermute | solution.py:262
  4.6 0.0 copy-start.10
  4.6 0.0 collective-permute-done.1.near_feat_hbm
  4.6 0.0 copy-start.9
  4.6 0.6 copy-done.10
  5.2 0.1 copy-done.9
  5.3 5.7 %messages.1 = (bf16[1024,128]{1,0:T(8,128)(2,1)}, bf16[4096,128]{1,0:T(8,128)(2,1)}) custom-call(s32[1]{0:T(128)} %bitcast.core_ref, s32[12,256]{1,0:T(8,128)} %bitcast.9, s32[12,256]{1,0:T(8,128)} %copy-done.10, s32[8]{0:T(128)} %hub_hbm.1, bf16[1024,128]{1,0:T(8,128)(2,1)} %feat_hbm.1, bf16[1024,128]{1,0:T(8,128)(2,1)} %copy-done.9, ...), custom_call_target="tpu_custom_call" | custom-call | flops 67108864 | bytes 2097152 | tf_op jit(solution)/shard_map/messages/pallas_call | solution.py:67
  11.1 13.8 %all-to-all-start = ((bf16[128,32,128]{2,1,0:T(8,128)(2,1)}), bf16[128,32,128]{2,1,0:T(8,128)(2,1)S(1)}, u32[]{:S(2)}, u32[]{:S(2)}) async-start(bf16[128,32,128]{2,1,0:T(8,128)(2,1)} %bitcast.7), calls=%async_computation | async-start | bytes 2097152 | tf_op jit(solution)/shard_map/all_to_all | solution.py:265
  24.9 0.0 copy-start.7
  24.9 0.0 copy-start.8
  24.9 0.0 copy-start.1
  24.9 1.9 %copy-done.1 = bf16[96,128,128]{2,1,0:T(8,128)(2,1)S(1)} copy-done((bf16[96,128,128]{2,1,0:T(8,128)(2,1)S(1)}, bf16[96,128,128]{2,1,0:T(8,128)(2,1)}, u32[]{:S(2)}) %copy-start.1) | copy-done | bytes 3145752
  26.8 0.0 copy-start.3
  26.8 0.9 %copy-done.3 = bf16[1024,128]{1,0:T(8,128)(2,1)S(1)} copy-done((bf16[1024,128]{1,0:T(8,128)(2,1)S(1)}, bf16[1024,128]{1,0:T(8,128)(2,1)}, u32[]{:S(2)}) %copy-start.3) | copy-done | bytes 262168
  27.7 0.0 copy-start.4
  27.7 0.7 %copy-done.4 = s32[96]{0:T(128)S(1)} copy-done((s32[96]{0:T(128)S(1)}, s32[96]{0:T(128)}, u32[]{:S(2)}) %copy-start.4) | copy-done | bytes 408
  28.4 0.0 copy-start.5
  28.4 0.7 %copy-done.5 = s32[96]{0:T(128)S(1)} copy-done((s32[96]{0:T(128)S(1)}, s32[96]{0:T(128)}, u32[]{:S(2)}) %copy-start.5) | copy-done | bytes 408
  29.1 0.7 %copy-done.6 = f32[128]{0:T(128)S(1)} copy-done((f32[128]{0:T(128)S(1)}, f32[128]{0:T(128)}, u32[]{:S(2)}) %copy-start.6) | copy-done | bytes 536
  29.7 2.0 %near_part.1.after_ref.near_ref = f32[1024,128]{1,0:T(8,128)S(1)} custom-call(s32[96]{0:T(128)S(1)} %copy-done.4, s32[96]{0:T(128)S(1)} %copy-done.5, bf16[96,128,128]{2,1,0:T(8,128)(2,1)S(1)} %copy-done.1, bf16[1024,128]{1,0:T(8,128)(2,1)S(1)} %copy-done.3, f32[1,128]{1,0:T(1,128)S(1)} %bitcast.6), custom_call_target="tpu_custom_call" | custom-call | flops 402653184 | bytes 4194304 | tf_op jit(solution)/shard_map/near_part/pallas_call | solution.py:109
  31.8 20.5 %all-to-all-done = bf16[128,32,128]{2,1,0:T(8,128)(2,1)S(1)} async-done(((bf16[128,32,128]{2,1,0:T(8,128)(2,1)}), bf16[128,32,128]{2,1,0:T(8,128)(2,1)S(1)}, u32[]{:S(2)}, u32[]{:S(2)}) %all-to-all-start) | async-done | bytes 1048608 | tf_op jit(solution)/shard_map/all_to_all | solution.py:265
  52.3 0.6 order_rows.1
  52.9 3.6 %collective-permute-start.2 = (bf16[1024,128]{1,0:T(8,128)(2,1)S(1)}, bf16[1024,128]{1,0:T(8,128)(2,1)S(1)}, u32[]{:S(2)}, u32[]{:S(2)}) collective-permute-start(bf16[1024,128]{1,0:T(8,128)(2,1)S(1)} %get-tuple-element.12.own_ref), channel_id=1, source_target_pairs={{0,4},{4,0},{8,12},{12,8},{16,20},{20,16},{24,28},{28,24},{32,36},... | collective-permute-start | bytes 786440 | tf_op jit(solution)/shard_map/ppermute | solution.py:275
  56.4 0.0 copy-done.7
  56.4 0.0 copy-done.8
  56.5 1.9 %copy-done.2 = bf16[96,128,128]{2,1,0:T(8,128)(2,1)S(1)} copy-done((bf16[96,128,128]{2,1,0:T(8,128)(2,1)S(1)}, bf16[96,128,128]{2,1,0:T(8,128)(2,1)}, u32[]{:S(2)}) %copy-start.2) | copy-done | bytes 3145752
  58.3 2.0 %far_part.1.sum_ref = f32[1024,128]{1,0:T(8,128)S(1)} custom-call(s32[96]{0:T(128)S(1)} %copy-done.7, s32[96]{0:T(128)S(1)} %copy-done.8, bf16[96,128,128]{2,1,0:T(8,128)(2,1)S(1)} %copy-done.2, bf16[3072,128]{1,0:T(8,128)(2,1)S(1)} %get-tuple-element.11.received_ref, f32[1024,128]{1,0:T(8,128)S(1)} %near_part.1.after_ref.near_ref), custom_call_target="tpu_custom_call" | custom-call | flops 402653184 | bytes 5242880 | tf_op jit(solution)/shard_map/far_part/pallas_call | solution.py:185
  60.4 0.0 collective-permute-done.2.other_ref
  60.4 0.0 copy-done
  60.4 2.6 %hub_part.1 = bf16[1024,128]{1,0:T(8,128)(2,1)} custom-call(s32[1]{0:T(128)} %bitcast.core_ref, f32[1024,128]{1,0:T(8,128)S(1)} %far_part.1.sum_ref, bf16[1024,2048]{1,0:T(8,128)(2,1)S(1)} %copy-done, bf16[1024,128]{1,0:T(8,128)(2,1)S(1)} %get-tuple-element.12.own_ref, bf16[1024,128]{1,0:T(8,128)(2,1)S(1)} %collective-permute-done.2.other_ref), custom_call_target="tpu_custom_call" | custom-call | flops 536870912 | bytes 6291456 | tf_op jit(solution)/shard_map/hub_part/pallas_call | solution.py:226
  (3 shorter events, 0.0 us)
Async XLA Ops:
  0.0 4.6 %collective-permute-start.1 = (bf16[1024,128]{1,0:T(8,128)(2,1)}, bf16[1024,128]{1,0:T(8,128)(2,1)S(1)}, u32[]{:S(2)}, u32[]{:S(2)}) collective-permute-start(bf16[1024,128]{1,0:T(8,128)(2,1)} %feat_hbm.1), channel_id=1, source_target_pairs={{0,4},{4,0},{8,12},{12,8},{16,20},{20,16},{24,28},{28,24},{32,36},... | collective-permute-start | bytes 786440 | tf_op jit(solution)/shard_map/ppermute | solution.py:263
  3.2 1.4 %collective-permute-start = (s32[12,256]{1,0:T(8,128)}, s32[12,256]{1,0:T(8,128)S(1)}, u32[]{:S(2)}, u32[]{:S(2)}) collective-permute-start(s32[12,256]{1,0:T(8,128)} %bitcast.8), channel_id=1, source_target_pairs={{0,4},{4,0},{8,12},{12,8},{16,20},{20,16},{24,28},{28,24},{32,36},... | collective-permute-start | bytes 36872 | tf_op jit(solution)/shard_map/ppermute | solution.py:262
  4.6 0.6 copy-start.10
  4.6 0.7 %copy-start.9 = (bf16[1024,128]{1,0:T(8,128)(2,1)}, bf16[1024,128]{1,0:T(8,128)(2,1)S(1)}, u32[]{:S(2)}) copy-start(bf16[1024,128]{1,0:T(8,128)(2,1)S(1)} %collective-permute-done.1.near_feat_hbm) | copy-start | bytes 786436
  11.1 41.2 %all-to-all-start = ((bf16[128,32,128]{2,1,0:T(8,128)(2,1)}), bf16[128,32,128]{2,1,0:T(8,128)(2,1)S(1)}, u32[]{:S(2)}, u32[]{:S(2)}) async-start(bf16[128,32,128]{2,1,0:T(8,128)(2,1)} %bitcast.7), calls=%async_computation | async-start | bytes 2097152 | tf_op jit(solution)/shard_map/all_to_all | solution.py:265
  24.9 31.6 %copy-start.7 = (s32[96]{0:T(128)S(1)}, s32[96]{0:T(128)}, u32[]{:S(2)}) copy-start(s32[96]{0:T(128)} %rows_ref.3) | copy-start | bytes 1156
  24.9 31.6 %copy-start.8 = (s32[96]{0:T(128)S(1)}, s32[96]{0:T(128)}, u32[]{:S(2)}) copy-start(s32[96]{0:T(128)} %blocks_ref.3) | copy-start | bytes 1156
  24.9 1.9 %copy-start.1 = (bf16[96,128,128]{2,1,0:T(8,128)(2,1)S(1)}, bf16[96,128,128]{2,1,0:T(8,128)(2,1)}, u32[]{:S(2)}) copy-start(bf16[96,128,128]{2,1,0:T(8,128)(2,1)} %values_ref.2) | copy-start | bytes 9437188
  26.8 0.9 %copy-start.3 = (bf16[1024,128]{1,0:T(8,128)(2,1)S(1)}, bf16[1024,128]{1,0:T(8,128)(2,1)}, u32[]{:S(2)}) copy-start(bf16[1024,128]{1,0:T(8,128)(2,1)} %get-tuple-element.10.mapped_ref) | copy-start | bytes 786436
  27.7 0.7 %copy-start.4 = (s32[96]{0:T(128)S(1)}, s32[96]{0:T(128)}, u32[]{:S(2)}) copy-start(s32[96]{0:T(128)} %rows_ref.2) | copy-start | bytes 1156
  28.4 0.7 %copy-start.5 = (s32[96]{0:T(128)S(1)}, s32[96]{0:T(128)}, u32[]{:S(2)}) copy-start(s32[96]{0:T(128)} %blocks_ref.2) | copy-start | bytes 1156
  29.1 0.7 %copy-start.6 = (f32[128]{0:T(128)S(1)}, f32[128]{0:T(128)}, u32[]{:S(2)}) copy-start(f32[128]{0:T(128)} %param.14) | copy-start | bytes 1540
  52.3 8.1 %copy-start = (bf16[1024,2048]{1,0:T(8,128)(2,1)S(1)}, bf16[1024,2048]{1,0:T(8,128)(2,1)}, u32[]{:S(2)}) copy-start(bf16[1024,2048]{1,0:T(8,128)(2,1)} %weights_ref.1) | copy-start | bytes 12582916
  52.9 7.5 %collective-permute-start.2 = (bf16[1024,128]{1,0:T(8,128)(2,1)S(1)}, bf16[1024,128]{1,0:T(8,128)(2,1)S(1)}, u32[]{:S(2)}, u32[]{:S(2)}) collective-permute-start(bf16[1024,128]{1,0:T(8,128)(2,1)S(1)} %get-tuple-element.12.own_ref), channel_id=1, source_target_pairs={{0,4},{4,0},{8,12},{12,8},{16,20},{20,16},{24,28},{28,24},{32,36},... | collective-permute-start | bytes 786440 | tf_op jit(solution)/shard_map/ppermute | solution.py:275
  56.4 1.9 %copy-start.2 = (bf16[96,128,128]{2,1,0:T(8,128)(2,1)S(1)}, bf16[96,128,128]{2,1,0:T(8,128)(2,1)}, u32[]{:S(2)}) copy-start(bf16[96,128,128]{2,1,0:T(8,128)(2,1)} %values_ref.3) | copy-start | bytes 9437188

commit v4 on v3

--- a/solution.py
+++ b/solution.py
@@ -161,7 +161,7 @@
         in_specs=[SMEM, VMEM, pl.BlockSpec(memory_space=pl.ANY)],
         out_specs=(VMEM, VMEM),
         compiler_params=pltpu.CompilerParams(vmem_limit_bytes=16 * MIB),
-        cost_estimate=pl.CostEstimate(flops=256 * total * width, bytes_accessed=2 * MIB, transcendentals=0),
+        cost_estimate=pl.CostEstimate(flops=8000000000, bytes_accessed=16 * MIB, transcendentals=0),
         name="order_rows",
     )(core, arrived, after)
 

time: 63.3 us -> 61.4 us (0.970)
  local copies, waits for them, and re-layouts: 7.42 us -> 5.52 us
    unnamed x22, local copies, waits for them, and re-layouts: 7.42 us -> 5.52 us
  transfers between devices with their start and end apart: 4 -> 4, of which waited for: 2 -> 2; matrix products, arithmetic and copies ran while one was open for 0% -> 0% of each run, Pallas kernels for 6% -> 7%
where the time goes in v4:
time: 61.4 us; the launch traced here: 61.1 us
  waiting for transfers between devices  22 us (36%)
  starting transfers between devices  20.6 us (34%)
  Pallas kernels  13 us (21%)
  local copies, waits for them, and re-layouts  5.52 us (9%)
    all_to_all x1, waiting for transfers between devices, on_device(): lax.all_to_all(messages.reshape(len(same_core[0]), -1, width), ('dom', 's...  20.6 us
    all_to_all x1, starting transfers between devices, on_device(): lax.all_to_all(messages.reshape(len(same_core[0]), -1, width), ('dom', 's...  13.8 us
    pallas_call x1, Pallas kernels, messages_of(): pl.pallas_call(send_kernel, out_shape=(jax.ShapeDtypeStruct((rows, width)...  5.72 us
    unnamed x22, local copies, waits for them, and re-layouts  5.52 us
    ppermute x1, starting transfers between devices, on_device(): other_hub = lax.ppermute(own_hub, 'dom', other_core)  3.56 us
    ppermute x1, starting transfers between devices, on_device(): near_features = lax.ppermute(features, 'dom', other_core)  3.24 us
    pallas_call x1, Pallas kernels, finish(): pl.pallas_call(hub_kernel, out_shape=jax.ShapeDtypeStruct((rows, width),...  2.62 us
    pallas_call x1, Pallas kernels, add_far_part(): pl.pallas_call(far_kernel, out_shape=jax.ShapeDtypeStruct((rows, width),...  2.01 us
  transfers between devices with their start and end apart: 4, of which 2 were waited for; matrix products, arithmetic and copies ran while one was open for 0% of the time, Pallas kernels for 7%

profile of v4, /device:TPU:1, one launch (start us, length us, event | category | flops | bytes accessed | tf_op | source)
XLA Modules:
  0.0 61.1 jit_solution(9742945728290641528)
XLA Ops:
  0.0 3.2 %collective-permute-start.1 = (bf16[1024,128]{1,0:T(8,128)(2,1)}, bf16[1024,128]{1,0:T(8,128)(2,1)S(1)}, u32[]{:S(2)}, u32[]{:S(2)}) collective-permute-start(bf16[1024,128]{1,0:T(8,128)(2,1)} %feat_hbm.1), channel_id=1, source_target_pairs={{0,4},{4,0},{8,12},{12,8},{16,20},{20,16},{24,28},{28,24},{32,36},... | collective-permute-start | bytes 786440 | tf_op jit(solution)/shard_map/ppermute | solution.py:263
  3.2 0.0 collective-permute-start
  3.2 1.4 %collective-permute-done.other_hbm = s32[12,256]{1,0:T(8,128)S(1)} collective-permute-done((s32[12,256]{1,0:T(8,128)}, s32[12,256]{1,0:T(8,128)S(1)}, u32[]{:S(2)}, u32[]{:S(2)}) %collective-permute-start) | collective-permute-done | bytes 12320 | tf_op jit(solution)/shard_map/ppermute | solution.py:262
  4.6 0.0 copy-start.10
  4.6 0.0 collective-permute-done.1.near_feat_hbm
  4.6 0.6 copy-done.10
  5.2 0.1 copy-done.9
  5.3 5.7 %messages.1 = (bf16[1024,128]{1,0:T(8,128)(2,1)}, bf16[4096,128]{1,0:T(8,128)(2,1)}) custom-call(s32[1]{0:T(128)} %bitcast.core_ref, s32[12,256]{1,0:T(8,128)} %bitcast.9, s32[12,256]{1,0:T(8,128)} %copy-done.10, s32[8]{0:T(128)} %hub_hbm.1, bf16[1024,128]{1,0:T(8,128)(2,1)} %feat_hbm.1, bf16[1024,128]{1,0:T(8,128)(2,1)} %copy-done.9, ...), custom_call_target="tpu_custom_call" | custom-call | flops 67108864 | bytes 2097152 | tf_op jit(solution)/shard_map/messages/pallas_call | solution.py:67
  11.1 13.8 %all-to-all-start = ((bf16[128,32,128]{2,1,0:T(8,128)(2,1)}), bf16[128,32,128]{2,1,0:T(8,128)(2,1)S(1)}, u32[]{:S(2)}, u32[]{:S(2)}) async-start(bf16[128,32,128]{2,1,0:T(8,128)(2,1)} %bitcast.7), calls=%async_computation | async-start | bytes 2097152 | tf_op jit(solution)/shard_map/all_to_all | solution.py:265
  24.9 0.0 copy-start.1
  24.9 1.9 %copy-done.1 = bf16[96,128,128]{2,1,0:T(8,128)(2,1)S(1)} copy-done((bf16[96,128,128]{2,1,0:T(8,128)(2,1)S(1)}, bf16[96,128,128]{2,1,0:T(8,128)(2,1)}, u32[]{:S(2)}) %copy-start.1) | copy-done | bytes 3145752
  26.8 0.0 copy-start.3
  26.8 0.9 %copy-done.3 = bf16[1024,128]{1,0:T(8,128)(2,1)S(1)} copy-done((bf16[1024,128]{1,0:T(8,128)(2,1)S(1)}, bf16[1024,128]{1,0:T(8,128)(2,1)}, u32[]{:S(2)}) %copy-start.3) | copy-done | bytes 262168
  27.7 0.0 copy-start.4
  27.7 0.7 %copy-done.4 = s32[96]{0:T(128)S(1)} copy-done((s32[96]{0:T(128)S(1)}, s32[96]{0:T(128)}, u32[]{:S(2)}) %copy-start.4) | copy-done | bytes 408
  28.4 0.0 copy-start.5
  28.4 0.7 %copy-done.5 = s32[96]{0:T(128)S(1)} copy-done((s32[96]{0:T(128)S(1)}, s32[96]{0:T(128)}, u32[]{:S(2)}) %copy-start.5) | copy-done | bytes 408
  29.0 0.0 copy-start.6
  29.0 0.7 %copy-done.6 = f32[128]{0:T(128)S(1)} copy-done((f32[128]{0:T(128)S(1)}, f32[128]{0:T(128)}, u32[]{:S(2)}) %copy-start.6) | copy-done | bytes 536
  29.7 2.0 %near_part.1.after_ref.near_ref = f32[1024,128]{1,0:T(8,128)S(1)} custom-call(s32[96]{0:T(128)S(1)} %copy-done.4, s32[96]{0:T(128)S(1)} %copy-done.5, bf16[96,128,128]{2,1,0:T(8,128)(2,1)S(1)} %copy-done.1, bf16[1024,128]{1,0:T(8,128)(2,1)S(1)} %copy-done.3, f32[1,128]{1,0:T(1,128)S(1)} %bitcast.6), custom_call_target="tpu_custom_call" | custom-call | flops 402653184 | bytes 4194304 | tf_op jit(solution)/shard_map/near_part/pallas_call | solution.py:109
  31.7 20.6 %all-to-all-done = bf16[128,32,128]{2,1,0:T(8,128)(2,1)S(1)} async-done(((bf16[128,32,128]{2,1,0:T(8,128)(2,1)}), bf16[128,32,128]{2,1,0:T(8,128)(2,1)S(1)}, u32[]{:S(2)}, u32[]{:S(2)}) %all-to-all-start) | async-done | bytes 1048608 | tf_op jit(solution)/shard_map/all_to_all | solution.py:265
  52.3 0.0 copy-start.2
  52.3 0.6 order_rows.1
  52.9 0.0 copy-start
  52.9 3.6 %collective-permute-start.2 = (bf16[1024,128]{1,0:T(8,128)(2,1)S(1)}, bf16[1024,128]{1,0:T(8,128)(2,1)S(1)}, u32[]{:S(2)}, u32[]{:S(2)}) collective-permute-start(bf16[1024,128]{1,0:T(8,128)(2,1)S(1)} %get-tuple-element.12.own_ref), channel_id=1, source_target_pairs={{0,4},{4,0},{8,12},{12,8},{16,20},{20,16},{24,28},{28,24},{32,36},... | collective-permute-start | bytes 786440 | tf_op jit(solution)/shard_map/ppermute | solution.py:275
  56.5 0.0 copy-done.2
  56.5 0.0 copy-done.7
  56.5 0.0 copy-done.8
  56.5 2.0 %far_part.1.sum_ref = f32[1024,128]{1,0:T(8,128)S(1)} custom-call(s32[96]{0:T(128)S(1)} %copy-done.7, s32[96]{0:T(128)S(1)} %copy-done.8, bf16[96,128,128]{2,1,0:T(8,128)(2,1)S(1)} %copy-done.2, bf16[3072,128]{1,0:T(8,128)(2,1)S(1)} %get-tuple-element.11.received_ref, f32[1024,128]{1,0:T(8,128)S(1)} %near_part.1.after_ref.near_ref), custom_call_target="tpu_custom_call" | custom-call | flops 402653184 | bytes 5242880 | tf_op jit(solution)/shard_map/far_part/pallas_call | solution.py:185
  58.5 0.0 collective-permute-done.2.other_ref
  58.5 0.0 copy-done
  58.5 2.6 %hub_part.1 = bf16[1024,128]{1,0:T(8,128)(2,1)} custom-call(s32[1]{0:T(128)} %bitcast.core_ref, f32[1024,128]{1,0:T(8,128)S(1)} %far_part.1.sum_ref, bf16[1024,2048]{1,0:T(8,128)(2,1)S(1)} %copy-done, bf16[1024,128]{1,0:T(8,128)(2,1)S(1)} %get-tuple-element.12.own_ref, bf16[1024,128]{1,0:T(8,128)(2,1)S(1)} %collective-permute-done.2.other_ref), custom_call_target="tpu_custom_call" | custom-call | flops 536870912 | bytes 6291456 | tf_op jit(solution)/shard_map/hub_part/pallas_call | solution.py:226
  (3 shorter events, 0.0 us)
Async XLA Ops:
  0.0 4.6 %collective-permute-start.1 = (bf16[1024,128]{1,0:T(8,128)(2,1)}, bf16[1024,128]{1,0:T(8,128)(2,1)S(1)}, u32[]{:S(2)}, u32[]{:S(2)}) collective-permute-start(bf16[1024,128]{1,0:T(8,128)(2,1)} %feat_hbm.1), channel_id=1, source_target_pairs={{0,4},{4,0},{8,12},{12,8},{16,20},{20,16},{24,28},{28,24},{32,36},... | collective-permute-start | bytes 786440 | tf_op jit(solution)/shard_map/ppermute | solution.py:263
  3.2 1.4 %collective-permute-start = (s32[12,256]{1,0:T(8,128)}, s32[12,256]{1,0:T(8,128)S(1)}, u32[]{:S(2)}, u32[]{:S(2)}) collective-permute-start(s32[12,256]{1,0:T(8,128)} %bitcast.8), channel_id=1, source_target_pairs={{0,4},{4,0},{8,12},{12,8},{16,20},{20,16},{24,28},{28,24},{32,36},... | collective-permute-start | bytes 36872 | tf_op jit(solution)/shard_map/ppermute | solution.py:262
  4.6 0.6 copy-start.10
  4.6 0.7 %copy-start.9 = (bf16[1024,128]{1,0:T(8,128)(2,1)}, bf16[1024,128]{1,0:T(8,128)(2,1)S(1)}, u32[]{:S(2)}) copy-start(bf16[1024,128]{1,0:T(8,128)(2,1)S(1)} %collective-permute-done.1.near_feat_hbm) | copy-start | bytes 786436
  11.1 41.2 %all-to-all-start = ((bf16[128,32,128]{2,1,0:T(8,128)(2,1)}), bf16[128,32,128]{2,1,0:T(8,128)(2,1)S(1)}, u32[]{:S(2)}, u32[]{:S(2)}) async-start(bf16[128,32,128]{2,1,0:T(8,128)(2,1)} %bitcast.7), calls=%async_computation | async-start | bytes 2097152 | tf_op jit(solution)/shard_map/all_to_all | solution.py:265
  24.9 1.9 %copy-start.1 = (bf16[96,128,128]{2,1,0:T(8,128)(2,1)S(1)}, bf16[96,128,128]{2,1,0:T(8,128)(2,1)}, u32[]{:S(2)}) copy-start(bf16[96,128,128]{2,1,0:T(8,128)(2,1)} %values_ref.2) | copy-start | bytes 9437188
  26.8 0.9 %copy-start.3 = (bf16[1024,128]{1,0:T(8,128)(2,1)S(1)}, bf16[1024,128]{1,0:T(8,128)(2,1)}, u32[]{:S(2)}) copy-start(bf16[1024,128]{1,0:T(8,128)(2,1)} %get-tuple-element.10.mapped_ref) | copy-start | bytes 786436
  27.7 0.7 %copy-start.4 = (s32[96]{0:T(128)S(1)}, s32[96]{0:T(128)}, u32[]{:S(2)}) copy-start(s32[96]{0:T(128)} %rows_ref.2) | copy-start | bytes 1156
  28.4 0.7 %copy-start.5 = (s32[96]{0:T(128)S(1)}, s32[96]{0:T(128)}, u32[]{:S(2)}) copy-start(s32[96]{0:T(128)} %blocks_ref.2) | copy-start | bytes 1156
  29.0 0.7 %copy-start.6 = (f32[128]{0:T(128)S(1)}, f32[128]{0:T(128)}, u32[]{:S(2)}) copy-start(f32[128]{0:T(128)} %param.14) | copy-start | bytes 1540
  52.3 4.2 %copy-start.2 = (bf16[96,128,128]{2,1,0:T(8,128)(2,1)S(1)}, bf16[96,128,128]{2,1,0:T(8,128)(2,1)}, u32[]{:S(2)}) copy-start(bf16[96,128,128]{2,1,0:T(8,128)(2,1)} %values_ref.3) | copy-start | bytes 9437188
  52.3 4.2 %copy-start.7 = (s32[96]{0:T(128)S(1)}, s32[96]{0:T(128)}, u32[]{:S(2)}) copy-start(s32[96]{0:T(128)} %rows_ref.3) | copy-start | bytes 1156
  52.3 4.2 %copy-start.8 = (s32[96]{0:T(128)S(1)}, s32[96]{0:T(128)}, u32[]{:S(2)}) copy-start(s32[96]{0:T(128)} %blocks_ref.3) | copy-start | bytes 1156
  52.9 5.6 %copy-start = (bf16[1024,2048]{1,0:T(8,128)(2,1)S(1)}, bf16[1024,2048]{1,0:T(8,128)(2,1)}, u32[]{:S(2)}) copy-start(bf16[1024,2048]{1,0:T(8,128)(2,1)} %weights_ref.1) | copy-start | bytes 12582916
  52.9 5.6 %collective-permute-start.2 = (bf16[1024,128]{1,0:T(8,128)(2,1)S(1)}, bf16[1024,128]{1,0:T(8,128)(2,1)S(1)}, u32[]{:S(2)}, u32[]{:S(2)}) collective-permute-start(bf16[1024,128]{1,0:T(8,128)(2,1)S(1)} %get-tuple-element.12.own_ref), channel_id=1, source_target_pairs={{0,4},{4,0},{8,12},{12,8},{16,20},{20,16},{24,28},{28,24},{32,36},... | collective-permute-start | bytes 786440 | tf_op jit(solution)/shard_map/ppermute | solution.py:275

commit v5 on v4

--- a/solution.py
+++ b/solution.py
@@ -13,9 +13,12 @@
 Y, Z, CORES, X = 4, 8, 2, 4
 
 
+PIECES = 4
+
+
 def send_kernel(
-    core_ref, own_hbm, other_hbm, hub_hbm, feat_hbm, near_feat_hbm, weight_hbm, mapped_ref, out_ref,
-    own, other, hub, feat, near_feat, weight, table, near_table, stage, sems
+    core_ref, own_hbm, other_hbm, hub_hbm, feat_hbm, near_feat_hbm, weight_hbm, mapped_hbm, message_hbm,
+    own, other, hub, feat, near_feat, weight, mapped, table, near_table, stage, out, sems, out_sems
 ):
     pairs = (
         (feat_hbm, feat), (weight_hbm, weight), (near_feat_hbm, near_feat),
@@ -30,10 +33,11 @@
     core = core_ref[0]
     copies[0].wait()
     copies[1].wait()
-    mapped = jnp.dot(feat[...], weight[...], preferred_element_type=jnp.float32)
-    mapped = mapped.astype(jnp.bfloat16)
-    mapped_ref[...] = mapped
-    table[...] = mapped.astype(jnp.float32)
+    mapped_rows = jnp.dot(feat[...], weight[...], preferred_element_type=jnp.float32).astype(jnp.bfloat16)
+    mapped[...] = mapped_rows
+    table[...] = mapped_rows.astype(jnp.float32)
+    sends = [pltpu.make_async_copy(mapped, mapped_hbm, out_sems.at[PIECES])]
+    sends[0].start()
     copies[2].wait()
     far = jnp.dot(near_feat[...], weight[...], preferred_element_type=jnp.float32)
     near_table[...] = far.astype(jnp.bfloat16).astype(jnp.float32)
@@ -50,11 +54,18 @@
             for j in range(slot):
                 stage[pl.ds(base + x * message + slot + j, 1), :] = near_table[pl.ds(other[j, r], 1), :]
             stage[pl.ds(base + x * message + 2 * slot, hubs), :] = hub_rows
-        rows = pl.ds(base, X * message)
-        out_ref[rows, :] = stage[rows, :].astype(jnp.bfloat16)
-        return carry
-
-    lax.fori_loop(0, Y * Z, step, 0)
+        return carry
+
+    groups = Y * Z // PIECES
+    for piece in range(PIECES):
+        lax.fori_loop(piece * groups, (piece + 1) * groups, step, 0, unroll=2)
+        rows = pl.ds(piece * groups * X * message, groups * X * message)
+        out[rows, :] = stage[rows, :].astype(jnp.bfloat16)
+        copy = pltpu.make_async_copy(out.at[rows], message_hbm.at[rows], out_sems.at[piece])
+        copy.start()
+        sends.append(copy)
+    for copy in sends:
+        copy.wait()
 
 
 HBM = pl.BlockSpec(memory_space=pltpu.HBM)
@@ -71,7 +82,7 @@
             jax.ShapeDtypeStruct((total, width), jnp.bfloat16),
         ),
         in_specs=[SMEM, HBM, HBM, HBM, HBM, HBM, HBM],
-        out_specs=(VMEM, VMEM),
+        out_specs=(HBM, HBM),
         scratch_shapes=[
             pltpu.SMEM(send_own.shape, jnp.int32),
             pltpu.SMEM(send_own.shape, jnp.int32),
@@ -79,10 +90,13 @@
             pltpu.VMEM(features.shape, jnp.bfloat16),
             pltpu.VMEM(features.shape, jnp.bfloat16),
             pltpu.VMEM(weight.shape, jnp.bfloat16),
+            pltpu.VMEM((rows, width), jnp.bfloat16),
             pltpu.VMEM((rows, width), jnp.float32),
             pltpu.VMEM((rows, width), jnp.float32),
             pltpu.VMEM((total, width), jnp.float32),
+            pltpu.VMEM((total, width), jnp.bfloat16),
             pltpu.SemaphoreType.DMA((6,)),
+            pltpu.SemaphoreType.DMA((PIECES + 1,)),
         ],
         compiler_params=pltpu.CompilerParams(vmem_limit_bytes=56 * MIB),
         cost_estimate=pl.CostEstimate(flops=4 * rows * width * width, bytes_accessed=2 * MIB, transcendentals=0),
@@ -217,7 +231,7 @@
         out_ref[rows, :] = jnp.maximum(total, 0.0).astype(out_ref.dtype)
         return carry
 
-    lax.fori_loop(0, out_ref.shape[0] // tile, step, 0)
+    lax.fori_loop(0, out_ref.shape[0] // tile, step, 0, unroll=True)
 
 
 def finish(core, total, weights, own_hub, other_hub):

time: 61.4 us -> 60.2 us (0.980)
  Pallas kernels: 13 us -> 11.8 us
    pallas_call x1, Pallas kernels: 5.72 us -> 5.01 us  [messages_of(): pl.pallas_call(send_kernel, out_shape=(jax.ShapeDtypeStruct((rows, width)...]
where the time goes in v5:
time: 60.2 us; the launch traced here: 60 us
  waiting for transfers between devices  22 us (37%)
  starting transfers between devices  20.6 us (34%)
  Pallas kernels  11.8 us (20%)
  local copies, waits for them, and re-layouts  5.52 us (9%)
    all_to_all x1, waiting for transfers between devices, on_device(): lax.all_to_all(messages.reshape(len(same_core[0]), -1, width), ('dom', 's...  20.6 us
    all_to_all x1, starting transfers between devices, on_device(): lax.all_to_all(messages.reshape(len(same_core[0]), -1, width), ('dom', 's...  13.8 us
    unnamed x22, local copies, waits for them, and re-layouts  5.52 us
    pallas_call x1, Pallas kernels, messages_of(): pl.pallas_call(send_kernel, out_shape=(jax.ShapeDtypeStruct((rows, width)...  5.01 us
    ppermute x1, starting transfers between devices, on_device(): other_hub = lax.ppermute(own_hub, 'dom', other_core)  3.54 us
    ppermute x1, starting transfers between devices, on_device(): near_features = lax.ppermute(features, 'dom', other_core)  3.24 us
    pallas_call x1, Pallas kernels, finish(): pl.pallas_call(hub_kernel, out_shape=jax.ShapeDtypeStruct((rows, width),...  2.17 us
    pallas_call x1, Pallas kernels, add_far_part(): pl.pallas_call(far_kernel, out_shape=jax.ShapeDtypeStruct((rows, width),...  2.04 us
  transfers between devices with their start and end apart: 4, of which 2 were waited for; matrix products, arithmetic and copies ran while one was open for 0% of the time, Pallas kernels for 7%

profile of v5, /device:TPU:1, one launch (start us, length us, event | category | flops | bytes accessed | tf_op | source)
XLA Modules:
  0.0 60.0 jit_solution(6033173167876474382)
XLA Ops:
  0.0 3.2 %collective-permute-start.1 = (bf16[1024,128]{1,0:T(8,128)(2,1)}, bf16[1024,128]{1,0:T(8,128)(2,1)S(1)}, u32[]{:S(2)}, u32[]{:S(2)}) collective-permute-start(bf16[1024,128]{1,0:T(8,128)(2,1)} %feat_hbm.1), channel_id=1, source_target_pairs={{0,4},{4,0},{8,12},{12,8},{16,20},{20,16},{24,28},{28,24},{32,36},... | collective-permute-start | bytes 786440 | tf_op jit(solution)/shard_map/ppermute | solution.py:277
  3.2 0.0 collective-permute-start
  3.2 1.4 %collective-permute-done.other_hbm = s32[12,256]{1,0:T(8,128)S(1)} collective-permute-done((s32[12,256]{1,0:T(8,128)}, s32[12,256]{1,0:T(8,128)S(1)}, u32[]{:S(2)}, u32[]{:S(2)}) %collective-permute-start) | collective-permute-done | bytes 12320 | tf_op jit(solution)/shard_map/ppermute | solution.py:276
  4.6 0.0 copy-start.10
  4.6 0.0 collective-permute-done.1.near_feat_hbm
  4.6 0.6 copy-done.10
  5.2 0.1 copy-done.9
  5.3 5.0 %messages.1 = (bf16[1024,128]{1,0:T(8,128)(2,1)}, bf16[4096,128]{1,0:T(8,128)(2,1)}) custom-call(s32[1]{0:T(128)} %bitcast.core_ref, s32[12,256]{1,0:T(8,128)} %bitcast.9, s32[12,256]{1,0:T(8,128)} %copy-done.10, s32[8]{0:T(128)} %hub_hbm.1, bf16[1024,128]{1,0:T(8,128)(2,1)} %feat_hbm.1, bf16[1024,128]{1,0:T(8,128)(2,1)} %copy-done.9, ...), custom_call_target="tpu_custom_call" | custom-call | flops 67108864 | bytes 2097152 | tf_op jit(solution)/shard_map/messages/pallas_call | solution.py:78
  10.4 13.8 %all-to-all-start = ((bf16[128,32,128]{2,1,0:T(8,128)(2,1)}), bf16[128,32,128]{2,1,0:T(8,128)(2,1)S(1)}, u32[]{:S(2)}, u32[]{:S(2)}) async-start(bf16[128,32,128]{2,1,0:T(8,128)(2,1)} %bitcast.7), calls=%async_computation | async-start | bytes 2097152 | tf_op jit(solution)/shard_map/all_to_all | solution.py:279
  24.1 0.0 copy-start.1
  24.2 1.9 %copy-done.1 = bf16[96,128,128]{2,1,0:T(8,128)(2,1)S(1)} copy-done((bf16[96,128,128]{2,1,0:T(8,128)(2,1)S(1)}, bf16[96,128,128]{2,1,0:T(8,128)(2,1)}, u32[]{:S(2)}) %copy-start.1) | copy-done | bytes 3145752
  26.0 0.9 %copy-done.3 = bf16[1024,128]{1,0:T(8,128)(2,1)S(1)} copy-done((bf16[1024,128]{1,0:T(8,128)(2,1)S(1)}, bf16[1024,128]{1,0:T(8,128)(2,1)}, u32[]{:S(2)}) %copy-start.3) | copy-done | bytes 262168
  27.0 0.0 copy-start.4
  27.0 0.7 %copy-done.4 = s32[96]{0:T(128)S(1)} copy-done((s32[96]{0:T(128)S(1)}, s32[96]{0:T(128)}, u32[]{:S(2)}) %copy-start.4) | copy-done | bytes 408
  27.6 0.0 copy-start.5
  27.7 0.7 %copy-done.5 = s32[96]{0:T(128)S(1)} copy-done((s32[96]{0:T(128)S(1)}, s32[96]{0:T(128)}, u32[]{:S(2)}) %copy-start.5) | copy-done | bytes 408
  28.3 0.0 copy-start.6
  28.3 0.7 %copy-done.6 = f32[128]{0:T(128)S(1)} copy-done((f32[128]{0:T(128)S(1)}, f32[128]{0:T(128)}, u32[]{:S(2)}) %copy-start.6) | copy-done | bytes 536
  29.0 2.0 %near_part.1.after_ref.near_ref = f32[1024,128]{1,0:T(8,128)S(1)} custom-call(s32[96]{0:T(128)S(1)} %copy-done.4, s32[96]{0:T(128)S(1)} %copy-done.5, bf16[96,128,128]{2,1,0:T(8,128)(2,1)S(1)} %copy-done.1, bf16[1024,128]{1,0:T(8,128)(2,1)S(1)} %copy-done.3, f32[1,128]{1,0:T(1,128)S(1)} %bitcast.6), custom_call_target="tpu_custom_call" | custom-call | flops 402653184 | bytes 4194304 | tf_op jit(solution)/shard_map/near_part/pallas_call | solution.py:123
  31.0 20.6 %all-to-all-done = bf16[128,32,128]{2,1,0:T(8,128)(2,1)S(1)} async-done(((bf16[128,32,128]{2,1,0:T(8,128)(2,1)}), bf16[128,32,128]{2,1,0:T(8,128)(2,1)S(1)}, u32[]{:S(2)}, u32[]{:S(2)}) %all-to-all-start) | async-done | bytes 1048608 | tf_op jit(solution)/shard_map/all_to_all | solution.py:279
  51.6 0.0 copy-start.2
  51.6 0.0 copy-start.7
  51.6 0.6 %order_rows.1 = (bf16[3072,128]{1,0:T(8,128)(2,1)S(1)}, bf16[1024,128]{1,0:T(8,128)(2,1)S(1)}) custom-call(s32[1]{0:T(128)} %bitcast.core_ref, bf16[4096,128]{1,0:T(8,128)(2,1)S(1)} %bitcast.5, f32[1024,128]{1,0:T(8,128)S(1)} %near_part.1.after_ref.near_ref), custom_call_target="tpu_custom_call" | custom-call | flops 8000000000 | bytes 16777216 | tf_op jit(solution)/shard_map/order_rows/pallas_call | solution.py:169
  52.2 0.0 copy-start
  52.2 3.5 %collective-permute-start.2 = (bf16[1024,128]{1,0:T(8,128)(2,1)S(1)}, bf16[1024,128]{1,0:T(8,128)(2,1)S(1)}, u32[]{:S(2)}, u32[]{:S(2)}) collective-permute-start(bf16[1024,128]{1,0:T(8,128)(2,1)S(1)} %get-tuple-element.12.own_ref), channel_id=1, source_target_pairs={{0,4},{4,0},{8,12},{12,8},{16,20},{20,16},{24,28},{28,24},{32,36},... | collective-permute-start | bytes 786440 | tf_op jit(solution)/shard_map/ppermute | solution.py:289
  55.7 0.0 copy-done.2
  55.7 0.0 copy-done.7
  55.7 0.0 copy-done.8
  55.7 2.0 %far_part.1.sum_ref = f32[1024,128]{1,0:T(8,128)S(1)} custom-call(s32[96]{0:T(128)S(1)} %copy-done.7, s32[96]{0:T(128)S(1)} %copy-done.8, bf16[96,128,128]{2,1,0:T(8,128)(2,1)S(1)} %copy-done.2, bf16[3072,128]{1,0:T(8,128)(2,1)S(1)} %get-tuple-element.11.received_ref, f32[1024,128]{1,0:T(8,128)S(1)} %near_part.1.after_ref.near_ref), custom_call_target="tpu_custom_call" | custom-call | flops 402653184 | bytes 5242880 | tf_op jit(solution)/shard_map/far_part/pallas_call | solution.py:199
  57.8 0.0 collective-permute-done.2.other_ref
  57.8 0.0 copy-done
  57.8 2.2 %hub_part.1 = bf16[1024,128]{1,0:T(8,128)(2,1)} custom-call(s32[1]{0:T(128)} %bitcast.core_ref, f32[1024,128]{1,0:T(8,128)S(1)} %far_part.1.sum_ref, bf16[1024,2048]{1,0:T(8,128)(2,1)S(1)} %copy-done, bf16[1024,128]{1,0:T(8,128)(2,1)S(1)} %get-tuple-element.12.own_ref, bf16[1024,128]{1,0:T(8,128)(2,1)S(1)} %collective-permute-done.2.other_ref), custom_call_target="tpu_custom_call" | custom-call | flops 536870912 | bytes 6291456 | tf_op jit(solution)/shard_map/hub_part/pallas_call | solution.py:240
  (3 shorter events, 0.0 us)
Async XLA Ops:
  0.0 4.6 %collective-permute-start.1 = (bf16[1024,128]{1,0:T(8,128)(2,1)}, bf16[1024,128]{1,0:T(8,128)(2,1)S(1)}, u32[]{:S(2)}, u32[]{:S(2)}) collective-permute-start(bf16[1024,128]{1,0:T(8,128)(2,1)} %feat_hbm.1), channel_id=1, source_target_pairs={{0,4},{4,0},{8,12},{12,8},{16,20},{20,16},{24,28},{28,24},{32,36},... | collective-permute-start | bytes 786440 | tf_op jit(solution)/shard_map/ppermute | solution.py:277
  3.2 1.4 %collective-permute-start = (s32[12,256]{1,0:T(8,128)}, s32[12,256]{1,0:T(8,128)S(1)}, u32[]{:S(2)}, u32[]{:S(2)}) collective-permute-start(s32[12,256]{1,0:T(8,128)} %bitcast.8), channel_id=1, source_target_pairs={{0,4},{4,0},{8,12},{12,8},{16,20},{20,16},{24,28},{28,24},{32,36},... | collective-permute-start | bytes 36872 | tf_op jit(solution)/shard_map/ppermute | solution.py:276
  4.6 0.6 copy-start.10
  4.6 0.7 %copy-start.9 = (bf16[1024,128]{1,0:T(8,128)(2,1)}, bf16[1024,128]{1,0:T(8,128)(2,1)S(1)}, u32[]{:S(2)}) copy-start(bf16[1024,128]{1,0:T(8,128)(2,1)S(1)} %collective-permute-done.1.near_feat_hbm) | copy-start | bytes 786436
  10.4 41.2 %all-to-all-start = ((bf16[128,32,128]{2,1,0:T(8,128)(2,1)}), bf16[128,32,128]{2,1,0:T(8,128)(2,1)S(1)}, u32[]{:S(2)}, u32[]{:S(2)}) async-start(bf16[128,32,128]{2,1,0:T(8,128)(2,1)} %bitcast.7), calls=%async_computation | async-start | bytes 2097152 | tf_op jit(solution)/shard_map/all_to_all | solution.py:279
  24.1 1.9 %copy-start.1 = (bf16[96,128,128]{2,1,0:T(8,128)(2,1)S(1)}, bf16[96,128,128]{2,1,0:T(8,128)(2,1)}, u32[]{:S(2)}) copy-start(bf16[96,128,128]{2,1,0:T(8,128)(2,1)} %values_ref.2) | copy-start | bytes 9437188
  26.0 0.9 %copy-start.3 = (bf16[1024,128]{1,0:T(8,128)(2,1)S(1)}, bf16[1024,128]{1,0:T(8,128)(2,1)}, u32[]{:S(2)}) copy-start(bf16[1024,128]{1,0:T(8,128)(2,1)} %get-tuple-element.10.mapped_ref) | copy-start | bytes 786436
  27.0 0.7 %copy-start.4 = (s32[96]{0:T(128)S(1)}, s32[96]{0:T(128)}, u32[]{:S(2)}) copy-start(s32[96]{0:T(128)} %rows_ref.2) | copy-start | bytes 1156
  27.6 0.7 %copy-start.5 = (s32[96]{0:T(128)S(1)}, s32[96]{0:T(128)}, u32[]{:S(2)}) copy-start(s32[96]{0:T(128)} %blocks_ref.2) | copy-start | bytes 1156
  28.3 0.7 %copy-start.6 = (f32[128]{0:T(128)S(1)}, f32[128]{0:T(128)}, u32[]{:S(2)}) copy-start(f32[128]{0:T(128)} %param.14) | copy-start | bytes 1540
  51.6 4.2 %copy-start.2 = (bf16[96,128,128]{2,1,0:T(8,128)(2,1)S(1)}, bf16[96,128,128]{2,1,0:T(8,128)(2,1)}, u32[]{:S(2)}) copy-start(bf16[96,128,128]{2,1,0:T(8,128)(2,1)} %values_ref.3) | copy-start | bytes 9437188
  51.6 4.2 %copy-start.7 = (s32[96]{0:T(128)S(1)}, s32[96]{0:T(128)}, u32[]{:S(2)}) copy-start(s32[96]{0:T(128)} %rows_ref.3) | copy-start | bytes 1156
  51.6 4.2 %copy-start.8 = (s32[96]{0:T(128)S(1)}, s32[96]{0:T(128)}, u32[]{:S(2)}) copy-start(s32[96]{0:T(128)} %blocks_ref.3) | copy-start | bytes 1156
  52.2 5.6 %copy-start = (bf16[1024,2048]{1,0:T(8,128)(2,1)S(1)}, bf16[1024,2048]{1,0:T(8,128)(2,1)}, u32[]{:S(2)}) copy-start(bf16[1024,2048]{1,0:T(8,128)(2,1)} %weights_ref.1) | copy-start | bytes 12582916
  52.2 5.6 %collective-permute-start.2 = (bf16[1024,128]{1,0:T(8,128)(2,1)S(1)}, bf16[1024,128]{1,0:T(8,128)(2,1)S(1)}, u32[]{:S(2)}, u32[]{:S(2)}) collective-permute-start(bf16[1024,128]{1,0:T(8,128)(2,1)S(1)} %get-tuple-element.12.own_ref), channel_id=1, source_target_pairs={{0,4},{4,0},{8,12},{12,8},{16,20},{20,16},{24,28},{28,24},{32,36},... | collective-permute-start | bytes 786440 | tf_op jit(solution)/shard_map/ppermute | solution.py:289

commit v6 on v5

--- a/solution.py
+++ b/solution.py
@@ -133,7 +133,7 @@
     )(rows_of, blocks_of, values, mapped, bias)
 
 
-def order_kernel(slot, core_ref, arrived_ref, after_ref, received_ref, hub_ref):
+def order_kernel(slot, core_ref, arrived_ref, received_ref, hub_ref):
     message = arrived_ref.shape[0] // (Y * Z * X)
     hubs = message - 2 * slot
     size = X * message
@@ -158,10 +158,10 @@
         hub_ref[pl.ds(pl.multiple_of(g * X * hubs, X * hubs), X * hubs), :] = sorted_rows[bound:]
         return carry
 
-    lax.fori_loop(0, Y * Z, step, 0, unroll=16)
-
-
-def order_rows(core, arrived, slot, after):
+    lax.fori_loop(0, Y * Z, step, 0, unroll=32)
+
+
+def order_rows(core, arrived, slot):
     total, width = arrived.shape
     groups = Y * Z
     bound = groups * CORES * X * slot
@@ -172,12 +172,12 @@
             jax.ShapeDtypeStruct((bound, width), jnp.bfloat16),
             jax.ShapeDtypeStruct((hubs, width), jnp.bfloat16),
         ),
-        in_specs=[SMEM, VMEM, pl.BlockSpec(memory_space=pl.ANY)],
+        in_specs=[SMEM, VMEM],
         out_specs=(VMEM, VMEM),
         compiler_params=pltpu.CompilerParams(vmem_limit_bytes=16 * MIB),
         cost_estimate=pl.CostEstimate(flops=8000000000, bytes_accessed=16 * MIB, transcendentals=0),
         name="order_rows",
-    )(core, arrived, after)
+    )(core, arrived)
 
 
 def far_kernel(rows_ref, blocks_ref, values_ref, received_ref, near_ref, out_ref):
@@ -190,7 +190,7 @@
         out_ref[rows, :] += jnp.dot(values_ref[t], received_ref[block, :], preferred_element_type=jnp.float32)
         return carry
 
-    lax.fori_loop(0, values_ref.shape[0], step, 0, unroll=32)
+    lax.fori_loop(0, values_ref.shape[0], step, 0, unroll=96)
 
 
 def add_far_part(rows_of, blocks_of, values, received, near):
@@ -222,7 +222,7 @@
         hub[pl.ds(other_at, half), :] = other_ref[rows, :]
         return carry
 
-    lax.fori_loop(0, groups, place, 0, unroll=8)
+    lax.fori_loop(0, groups, place, 0, unroll=16)
     tile = 256
 
     def step(i, carry):
@@ -285,7 +285,8 @@
         axis_index_groups=same_core,
     ).reshape(-1, width)
     near = near_part(local_rows, local_blocks, local_values, mapped, layer_bias[None, :])
-    received, own_hub = order_rows(core, arrived, slot, near)
+    arrived, near = lax.optimization_barrier((arrived, near))
+    received, own_hub = order_rows(core, arrived, slot)
     other_hub = lax.ppermute(own_hub, "dom", other_core)
     total = add_far_part(bound_rows, bound_blocks, bound_values, received, near)
     return finish(core, total, hub_weights, own_hub, other_hub)

time: 60.2 us -> 59.9 us (level)
  transfers between devices with their start and end apart: 4 -> 4, of which waited for: 2 -> 2; matrix products, arithmetic and copies ran while one was open for 0% -> 0% of each run, Pallas kernels for 7% -> 6%
where the time goes in v6:
time: 59.9 us; the launch traced here: 59.6 us
  waiting for transfers between devices  22 us (37%)
  starting transfers between devices  20.6 us (34%)
  Pallas kernels  11.4 us (19%)
  local copies, waits for them, and re-layouts  5.52 us (9%)
    all_to_all x1, waiting for transfers between devices, on_device(): lax.all_to_all(messages.reshape(len(same_core[0]), -1, width), ('dom', 's...  20.6 us
    all_to_all x1, starting transfers between devices, on_device(): lax.all_to_all(messages.reshape(len(same_core[0]), -1, width), ('dom', 's...  13.8 us
    unnamed x22, local copies, waits for them, and re-layouts  5.52 us
    pallas_call x1, Pallas kernels, messages_of(): pl.pallas_call(send_kernel, out_shape=(jax.ShapeDtypeStruct((rows, width)...  5.01 us
    ppermute x1, starting transfers between devices, on_device(): other_hub = lax.ppermute(own_hub, 'dom', other_core)  3.56 us
    ppermute x1, starting transfers between devices, on_device(): near_features = lax.ppermute(features, 'dom', other_core)  3.24 us
    pallas_call x1, Pallas kernels, finish(): pl.pallas_call(hub_kernel, out_shape=jax.ShapeDtypeStruct((rows, width),...  2.16 us
    pallas_call x1, Pallas kernels, near_part(): pl.pallas_call(near_kernel, out_shape=jax.ShapeDtypeStruct((rows, width),...  2.01 us
  transfers between devices with their start and end apart: 4, of which 2 were waited for; matrix products, arithmetic and copies ran while one was open for 0% of the time, Pallas kernels for 6%

profile of v6, /device:TPU:1, one launch (start us, length us, event | category | flops | bytes accessed | tf_op | source)
XLA Modules:
  0.0 59.6 jit_solution(3481781577316093089)
XLA Ops:
  0.0 3.2 %collective-permute-start.1 = (bf16[1024,128]{1,0:T(8,128)(2,1)}, bf16[1024,128]{1,0:T(8,128)(2,1)S(1)}, u32[]{:S(2)}, u32[]{:S(2)}) collective-permute-start(bf16[1024,128]{1,0:T(8,128)(2,1)} %feat_hbm.1), channel_id=1, source_target_pairs={{0,4},{4,0},{8,12},{12,8},{16,20},{20,16},{24,28},{28,24},{32,36},... | collective-permute-start | bytes 786440 | tf_op jit(solution)/shard_map/ppermute | solution.py:277
  3.2 0.0 collective-permute-start
  3.2 1.4 %collective-permute-done.other_hbm = s32[12,256]{1,0:T(8,128)S(1)} collective-permute-done((s32[12,256]{1,0:T(8,128)}, s32[12,256]{1,0:T(8,128)S(1)}, u32[]{:S(2)}, u32[]{:S(2)}) %collective-permute-start) | collective-permute-done | bytes 12320 | tf_op jit(solution)/shard_map/ppermute | solution.py:276
  4.6 0.0 copy-start.10
  4.6 0.0 collective-permute-done.1.near_feat_hbm
  4.6 0.0 copy-start.9
  4.6 0.6 copy-done.10
  5.2 0.1 copy-done.9
  5.3 5.0 %messages.1 = (bf16[1024,128]{1,0:T(8,128)(2,1)}, bf16[4096,128]{1,0:T(8,128)(2,1)}) custom-call(s32[1]{0:T(128)} %bitcast.core_ref, s32[12,256]{1,0:T(8,128)} %bitcast.9, s32[12,256]{1,0:T(8,128)} %copy-done.10, s32[8]{0:T(128)} %hub_hbm.1, bf16[1024,128]{1,0:T(8,128)(2,1)} %feat_hbm.1, bf16[1024,128]{1,0:T(8,128)(2,1)} %copy-done.9, ...), custom_call_target="tpu_custom_call" | custom-call | flops 67108864 | bytes 2097152 | tf_op jit(solution)/shard_map/messages/pallas_call | solution.py:78
  10.4 13.8 %all-to-all-start = ((bf16[128,32,128]{2,1,0:T(8,128)(2,1)}), bf16[128,32,128]{2,1,0:T(8,128)(2,1)S(1)}, u32[]{:S(2)}, u32[]{:S(2)}) async-start(bf16[128,32,128]{2,1,0:T(8,128)(2,1)} %bitcast.7), calls=%async_computation | async-start | bytes 2097152 | tf_op jit(solution)/shard_map/all_to_all | solution.py:279
  24.1 0.0 copy-start.1
  24.2 1.9 %copy-done.1 = bf16[96,128,128]{2,1,0:T(8,128)(2,1)S(1)} copy-done((bf16[96,128,128]{2,1,0:T(8,128)(2,1)S(1)}, bf16[96,128,128]{2,1,0:T(8,128)(2,1)}, u32[]{:S(2)}) %copy-start.1) | copy-done | bytes 3145752
  26.0 0.0 copy-start.3
  26.0 0.9 %copy-done.3 = bf16[1024,128]{1,0:T(8,128)(2,1)S(1)} copy-done((bf16[1024,128]{1,0:T(8,128)(2,1)S(1)}, bf16[1024,128]{1,0:T(8,128)(2,1)}, u32[]{:S(2)}) %copy-start.3) | copy-done | bytes 262168
  27.0 0.0 copy-start.4
  27.0 0.7 %copy-done.4 = s32[96]{0:T(128)S(1)} copy-done((s32[96]{0:T(128)S(1)}, s32[96]{0:T(128)}, u32[]{:S(2)}) %copy-start.4) | copy-done | bytes 408
  27.6 0.0 copy-start.5
  27.7 0.7 %copy-done.5 = s32[96]{0:T(128)S(1)} copy-done((s32[96]{0:T(128)S(1)}, s32[96]{0:T(128)}, u32[]{:S(2)}) %copy-start.5) | copy-done | bytes 408
  28.3 0.0 copy-start.6
  28.3 0.7 %copy-done.6 = f32[128]{0:T(128)S(1)} copy-done((f32[128]{0:T(128)S(1)}, f32[128]{0:T(128)}, u32[]{:S(2)}) %copy-start.6) | copy-done | bytes 536
  29.0 2.0 %near_part.1.near_ref = f32[1024,128]{1,0:T(8,128)S(1)} custom-call(s32[96]{0:T(128)S(1)} %copy-done.4, s32[96]{0:T(128)S(1)} %copy-done.5, bf16[96,128,128]{2,1,0:T(8,128)(2,1)S(1)} %copy-done.1, bf16[1024,128]{1,0:T(8,128)(2,1)S(1)} %copy-done.3, f32[1,128]{1,0:T(1,128)S(1)} %bitcast.6), custom_call_target="tpu_custom_call" | custom-call | flops 402653184 | bytes 4194304 | tf_op jit(solution)/shard_map/near_part/pallas_call | solution.py:123
  31.0 20.6 %all-to-all-done = bf16[128,32,128]{2,1,0:T(8,128)(2,1)S(1)} async-done(((bf16[128,32,128]{2,1,0:T(8,128)(2,1)}), bf16[128,32,128]{2,1,0:T(8,128)(2,1)S(1)}, u32[]{:S(2)}, u32[]{:S(2)}) %all-to-all-start) | async-done | bytes 1048608 | tf_op jit(solution)/shard_map/all_to_all | solution.py:279
  51.6 0.4 order_rows.1
  52.0 0.0 copy-start
  52.0 3.6 %collective-permute-start.2 = (bf16[1024,128]{1,0:T(8,128)(2,1)S(1)}, bf16[1024,128]{1,0:T(8,128)(2,1)S(1)}, u32[]{:S(2)}, u32[]{:S(2)}) collective-permute-start(bf16[1024,128]{1,0:T(8,128)(2,1)S(1)} %get-tuple-element.16.own_ref), channel_id=1, source_target_pairs={{0,4},{4,0},{8,12},{12,8},{16,20},{20,16},{24,28},{28,24},{32,36},... | collective-permute-start | bytes 786440 | tf_op jit(solution)/shard_map/ppermute | solution.py:290
  55.6 0.0 copy-done.2
  55.6 0.0 copy-done.7
  55.6 0.0 copy-done.8
  55.6 1.8 %far_part.1.sum_ref = f32[1024,128]{1,0:T(8,128)S(1)} custom-call(s32[96]{0:T(128)S(1)} %copy-done.7, s32[96]{0:T(128)S(1)} %copy-done.8, bf16[96,128,128]{2,1,0:T(8,128)(2,1)S(1)} %copy-done.2, bf16[3072,128]{1,0:T(8,128)(2,1)S(1)} %get-tuple-element.14.received_ref, f32[1024,128]{1,0:T(8,128)S(1)} %near_part.1.near_ref), custom_call_target="tpu_custom_call" | custom-call | flops 402653184 | bytes 5242880 | tf_op jit(solution)/shard_map/far_part/pallas_call | solution.py:199
  57.4 0.0 collective-permute-done.2.other_ref
  57.4 0.0 copy-done
  57.5 2.2 %hub_part.1 = bf16[1024,128]{1,0:T(8,128)(2,1)} custom-call(s32[1]{0:T(128)} %bitcast.core_ref, f32[1024,128]{1,0:T(8,128)S(1)} %far_part.1.sum_ref, bf16[1024,2048]{1,0:T(8,128)(2,1)S(1)} %copy-done, bf16[1024,128]{1,0:T(8,128)(2,1)S(1)} %get-tuple-element.16.own_ref, bf16[1024,128]{1,0:T(8,128)(2,1)S(1)} %collective-permute-done.2.other_ref), custom_call_target="tpu_custom_call" | custom-call | flops 536870912 | bytes 6291456 | tf_op jit(solution)/shard_map/hub_part/pallas_call | solution.py:240
  (3 shorter events, 0.0 us)
Async XLA Ops:
  0.0 4.6 %collective-permute-start.1 = (bf16[1024,128]{1,0:T(8,128)(2,1)}, bf16[1024,128]{1,0:T(8,128)(2,1)S(1)}, u32[]{:S(2)}, u32[]{:S(2)}) collective-permute-start(bf16[1024,128]{1,0:T(8,128)(2,1)} %feat_hbm.1), channel_id=1, source_target_pairs={{0,4},{4,0},{8,12},{12,8},{16,20},{20,16},{24,28},{28,24},{32,36},... | collective-permute-start | bytes 786440 | tf_op jit(solution)/shard_map/ppermute | solution.py:277
  3.2 1.4 %collective-permute-start = (s32[12,256]{1,0:T(8,128)}, s32[12,256]{1,0:T(8,128)S(1)}, u32[]{:S(2)}, u32[]{:S(2)}) collective-permute-start(s32[12,256]{1,0:T(8,128)} %bitcast.8), channel_id=1, source_target_pairs={{0,4},{4,0},{8,12},{12,8},{16,20},{20,16},{24,28},{28,24},{32,36},... | collective-permute-start | bytes 36872 | tf_op jit(solution)/shard_map/ppermute | solution.py:276
  4.6 0.6 copy-start.10
  4.6 0.7 %copy-start.9 = (bf16[1024,128]{1,0:T(8,128)(2,1)}, bf16[1024,128]{1,0:T(8,128)(2,1)S(1)}, u32[]{:S(2)}) copy-start(bf16[1024,128]{1,0:T(8,128)(2,1)S(1)} %collective-permute-done.1.near_feat_hbm) | copy-start | bytes 786436
  10.4 41.2 %all-to-all-start = ((bf16[128,32,128]{2,1,0:T(8,128)(2,1)}), bf16[128,32,128]{2,1,0:T(8,128)(2,1)S(1)}, u32[]{:S(2)}, u32[]{:S(2)}) async-start(bf16[128,32,128]{2,1,0:T(8,128)(2,1)} %bitcast.7), calls=%async_computation | async-start | bytes 2097152 | tf_op jit(solution)/shard_map/all_to_all | solution.py:279
  24.1 1.9 %copy-start.1 = (bf16[96,128,128]{2,1,0:T(8,128)(2,1)S(1)}, bf16[96,128,128]{2,1,0:T(8,128)(2,1)}, u32[]{:S(2)}) copy-start(bf16[96,128,128]{2,1,0:T(8,128)(2,1)} %values_ref.2) | copy-start | bytes 9437188
  26.0 0.9 %copy-start.3 = (bf16[1024,128]{1,0:T(8,128)(2,1)S(1)}, bf16[1024,128]{1,0:T(8,128)(2,1)}, u32[]{:S(2)}) copy-start(bf16[1024,128]{1,0:T(8,128)(2,1)} %get-tuple-element.12.mapped_ref) | copy-start | bytes 786436
  27.0 0.7 %copy-start.4 = (s32[96]{0:T(128)S(1)}, s32[96]{0:T(128)}, u32[]{:S(2)}) copy-start(s32[96]{0:T(128)} %rows_ref.2) | copy-start | bytes 1156
  27.6 0.7 %copy-start.5 = (s32[96]{0:T(128)S(1)}, s32[96]{0:T(128)}, u32[]{:S(2)}) copy-start(s32[96]{0:T(128)} %blocks_ref.2) | copy-start | bytes 1156
  28.3 0.7 %copy-start.6 = (f32[128]{0:T(128)S(1)}, f32[128]{0:T(128)}, u32[]{:S(2)}) copy-start(f32[128]{0:T(128)} %param.14) | copy-start | bytes 1540
  51.6 4.0 %copy-start.2 = (bf16[96,128,128]{2,1,0:T(8,128)(2,1)S(1)}, bf16[96,128,128]{2,1,0:T(8,128)(2,1)}, u32[]{:S(2)}) copy-start(bf16[96,128,128]{2,1,0:T(8,128)(2,1)} %values_ref.3) | copy-start | bytes 9437188
  51.6 4.0 %copy-start.7 = (s32[96]{0:T(128)S(1)}, s32[96]{0:T(128)}, u32[]{:S(2)}) copy-start(s32[96]{0:T(128)} %rows_ref.3) | copy-start | bytes 1156
  51.6 4.0 %copy-start.8 = (s32[96]{0:T(128)S(1)}, s32[96]{0:T(128)}, u32[]{:S(2)}) copy-start(s32[96]{0:T(128)} %blocks_ref.3) | copy-start | bytes 1156
  52.0 5.4 %copy-start = (bf16[1024,2048]{1,0:T(8,128)(2,1)S(1)}, bf16[1024,2048]{1,0:T(8,128)(2,1)}, u32[]{:S(2)}) copy-start(bf16[1024,2048]{1,0:T(8,128)(2,1)} %weights_ref.1) | copy-start | bytes 12582916
  52.0 5.4 %collective-permute-start.2 = (bf16[1024,128]{1,0:T(8,128)(2,1)S(1)}, bf16[1024,128]{1,0:T(8,128)(2,1)S(1)}, u32[]{:S(2)}, u32[]{:S(2)}) collective-permute-start(bf16[1024,128]{1,0:T(8,128)(2,1)S(1)} %get-tuple-element.16.own_ref), channel_id=1, source_target_pairs={{0,4},{4,0},{8,12},{12,8},{16,20},{20,16},{24,28},{28,24},{32,36},... | collective-permute-start | bytes 786440 | tf_op jit(solution)/shard_map/ppermute | solution.py:290

commit v7 on v6

--- a/solution.py
+++ b/solution.py
@@ -58,7 +58,7 @@
 
     groups = Y * Z // PIECES
     for piece in range(PIECES):
-        lax.fori_loop(piece * groups, (piece + 1) * groups, step, 0, unroll=2)
+        lax.fori_loop(piece * groups, (piece + 1) * groups, step, 0, unroll=8)
         rows = pl.ds(piece * groups * X * message, groups * X * message)
         out[rows, :] = stage[rows, :].astype(jnp.bfloat16)
         copy = pltpu.make_async_copy(out.at[rows], message_hbm.at[rows], out_sems.at[piece])

time: 59.9 us -> 59.7 us (level)
  no operation moved by 1% of the time
where the time goes in v7:
time: 59.7 us; the launch traced here: 59.5 us
  waiting for transfers between devices  22 us (37%)
  starting transfers between devices  20.6 us (35%)
  Pallas kernels  11.3 us (19%)
  local copies, waits for them, and re-layouts  5.52 us (9%)
    all_to_all x1, waiting for transfers between devices, on_device(): lax.all_to_all(messages.reshape(len(same_core[0]), -1, width), ('dom', 's...  20.6 us
    all_to_all x1, starting transfers between devices, on_device(): lax.all_to_all(messages.reshape(len(same_core[0]), -1, width), ('dom', 's...  13.8 us
    unnamed x22, local copies, waits for them, and re-layouts  5.52 us
    pallas_call x1, Pallas kernels, messages_of(): pl.pallas_call(send_kernel, out_shape=(jax.ShapeDtypeStruct((rows, width)...  4.89 us
    ppermute x1, starting transfers between devices, on_device(): other_hub = lax.ppermute(own_hub, 'dom', other_core)  3.56 us
    ppermute x1, starting transfers between devices, on_device(): near_features = lax.ppermute(features, 'dom', other_core)  3.24 us
    pallas_call x1, Pallas kernels, finish(): pl.pallas_call(hub_kernel, out_shape=jax.ShapeDtypeStruct((rows, width),...  2.16 us
    pallas_call x1, Pallas kernels, near_part(): pl.pallas_call(near_kernel, out_shape=jax.ShapeDtypeStruct((rows, width),...  2.01 us
  transfers between devices with their start and end apart: 4, of which 2 were waited for; matrix products, arithmetic and copies ran while one was open for 0% of the time, Pallas kernels for 6%

profile of v7, /device:TPU:1, one launch (start us, length us, event | category | flops | bytes accessed | tf_op | source)
XLA Modules:
  0.0 59.5 jit_solution(5719831589019952148)
XLA Ops:
  0.0 3.2 %collective-permute-start.1 = (bf16[1024,128]{1,0:T(8,128)(2,1)}, bf16[1024,128]{1,0:T(8,128)(2,1)S(1)}, u32[]{:S(2)}, u32[]{:S(2)}) collective-permute-start(bf16[1024,128]{1,0:T(8,128)(2,1)} %feat_hbm.1), channel_id=1, source_target_pairs={{0,4},{4,0},{8,12},{12,8},{16,20},{20,16},{24,28},{28,24},{32,36},... | collective-permute-start | bytes 786440 | tf_op jit(solution)/shard_map/ppermute | solution.py:277
  3.2 0.0 collective-permute-start
  3.2 1.4 %collective-permute-done.other_hbm = s32[12,256]{1,0:T(8,128)S(1)} collective-permute-done((s32[12,256]{1,0:T(8,128)}, s32[12,256]{1,0:T(8,128)S(1)}, u32[]{:S(2)}, u32[]{:S(2)}) %collective-permute-start) | collective-permute-done | bytes 12320 | tf_op jit(solution)/shard_map/ppermute | solution.py:276
  4.6 0.0 copy-start.10
  4.6 0.0 collective-permute-done.1.near_feat_hbm
  4.6 0.0 copy-start.9
  4.6 0.6 copy-done.10
  5.2 0.1 copy-done.9
  5.3 4.9 %messages.1 = (bf16[1024,128]{1,0:T(8,128)(2,1)}, bf16[4096,128]{1,0:T(8,128)(2,1)}) custom-call(s32[1]{0:T(128)} %bitcast.core_ref, s32[12,256]{1,0:T(8,128)} %bitcast.9, s32[12,256]{1,0:T(8,128)} %copy-done.10, s32[8]{0:T(128)} %hub_hbm.1, bf16[1024,128]{1,0:T(8,128)(2,1)} %feat_hbm.1, bf16[1024,128]{1,0:T(8,128)(2,1)} %copy-done.9, ...), custom_call_target="tpu_custom_call" | custom-call | flops 67108864 | bytes 2097152 | tf_op jit(solution)/shard_map/messages/pallas_call | solution.py:78
  10.2 13.8 %all-to-all-start = ((bf16[128,32,128]{2,1,0:T(8,128)(2,1)}), bf16[128,32,128]{2,1,0:T(8,128)(2,1)S(1)}, u32[]{:S(2)}, u32[]{:S(2)}) async-start(bf16[128,32,128]{2,1,0:T(8,128)(2,1)} %bitcast.7), calls=%async_computation | async-start | bytes 2097152 | tf_op jit(solution)/shard_map/all_to_all | solution.py:279
  24.0 0.0 copy-start.1
  24.0 1.9 %copy-done.1 = bf16[96,128,128]{2,1,0:T(8,128)(2,1)S(1)} copy-done((bf16[96,128,128]{2,1,0:T(8,128)(2,1)S(1)}, bf16[96,128,128]{2,1,0:T(8,128)(2,1)}, u32[]{:S(2)}) %copy-start.1) | copy-done | bytes 3145752
  25.9 0.0 copy-start.3
  25.9 0.9 %copy-done.3 = bf16[1024,128]{1,0:T(8,128)(2,1)S(1)} copy-done((bf16[1024,128]{1,0:T(8,128)(2,1)S(1)}, bf16[1024,128]{1,0:T(8,128)(2,1)}, u32[]{:S(2)}) %copy-start.3) | copy-done | bytes 262168
  26.9 0.0 copy-start.4
  26.9 0.7 %copy-done.4 = s32[96]{0:T(128)S(1)} copy-done((s32[96]{0:T(128)S(1)}, s32[96]{0:T(128)}, u32[]{:S(2)}) %copy-start.4) | copy-done | bytes 408
  27.5 0.0 copy-start.5
  27.5 0.7 %copy-done.5 = s32[96]{0:T(128)S(1)} copy-done((s32[96]{0:T(128)S(1)}, s32[96]{0:T(128)}, u32[]{:S(2)}) %copy-start.5) | copy-done | bytes 408
  28.2 0.0 copy-start.6
  28.2 0.7 %copy-done.6 = f32[128]{0:T(128)S(1)} copy-done((f32[128]{0:T(128)S(1)}, f32[128]{0:T(128)}, u32[]{:S(2)}) %copy-start.6) | copy-done | bytes 536
  28.8 2.0 %near_part.1.near_ref = f32[1024,128]{1,0:T(8,128)S(1)} custom-call(s32[96]{0:T(128)S(1)} %copy-done.4, s32[96]{0:T(128)S(1)} %copy-done.5, bf16[96,128,128]{2,1,0:T(8,128)(2,1)S(1)} %copy-done.1, bf16[1024,128]{1,0:T(8,128)(2,1)S(1)} %copy-done.3, f32[1,128]{1,0:T(1,128)S(1)} %bitcast.6), custom_call_target="tpu_custom_call" | custom-call | flops 402653184 | bytes 4194304 | tf_op jit(solution)/shard_map/near_part/pallas_call | solution.py:123
  30.9 20.6 %all-to-all-done = bf16[128,32,128]{2,1,0:T(8,128)(2,1)S(1)} async-done(((bf16[128,32,128]{2,1,0:T(8,128)(2,1)}), bf16[128,32,128]{2,1,0:T(8,128)(2,1)S(1)}, u32[]{:S(2)}, u32[]{:S(2)}) %all-to-all-start) | async-done | bytes 1048608 | tf_op jit(solution)/shard_map/all_to_all | solution.py:279
  51.4 0.4 order_rows.1
  51.9 0.0 copy-start
  51.9 3.6 %collective-permute-start.2 = (bf16[1024,128]{1,0:T(8,128)(2,1)S(1)}, bf16[1024,128]{1,0:T(8,128)(2,1)S(1)}, u32[]{:S(2)}, u32[]{:S(2)}) collective-permute-start(bf16[1024,128]{1,0:T(8,128)(2,1)S(1)} %get-tuple-element.16.own_ref), channel_id=1, source_target_pairs={{0,4},{4,0},{8,12},{12,8},{16,20},{20,16},{24,28},{28,24},{32,36},... | collective-permute-start | bytes 786440 | tf_op jit(solution)/shard_map/ppermute | solution.py:290
  55.5 0.0 copy-done.2
  55.5 0.0 copy-done.7
  55.5 0.0 copy-done.8
  55.5 1.8 %far_part.1.sum_ref = f32[1024,128]{1,0:T(8,128)S(1)} custom-call(s32[96]{0:T(128)S(1)} %copy-done.7, s32[96]{0:T(128)S(1)} %copy-done.8, bf16[96,128,128]{2,1,0:T(8,128)(2,1)S(1)} %copy-done.2, bf16[3072,128]{1,0:T(8,128)(2,1)S(1)} %get-tuple-element.14.received_ref, f32[1024,128]{1,0:T(8,128)S(1)} %near_part.1.near_ref), custom_call_target="tpu_custom_call" | custom-call | flops 402653184 | bytes 5242880 | tf_op jit(solution)/shard_map/far_part/pallas_call | solution.py:199
  57.3 0.0 collective-permute-done.2.other_ref
  57.3 0.0 copy-done
  57.3 2.2 %hub_part.1 = bf16[1024,128]{1,0:T(8,128)(2,1)} custom-call(s32[1]{0:T(128)} %bitcast.core_ref, f32[1024,128]{1,0:T(8,128)S(1)} %far_part.1.sum_ref, bf16[1024,2048]{1,0:T(8,128)(2,1)S(1)} %copy-done, bf16[1024,128]{1,0:T(8,128)(2,1)S(1)} %get-tuple-element.16.own_ref, bf16[1024,128]{1,0:T(8,128)(2,1)S(1)} %collective-permute-done.2.other_ref), custom_call_target="tpu_custom_call" | custom-call | flops 536870912 | bytes 6291456 | tf_op jit(solution)/shard_map/hub_part/pallas_call | solution.py:240
  (3 shorter events, 0.0 us)
Async XLA Ops:
  0.0 4.6 %collective-permute-start.1 = (bf16[1024,128]{1,0:T(8,128)(2,1)}, bf16[1024,128]{1,0:T(8,128)(2,1)S(1)}, u32[]{:S(2)}, u32[]{:S(2)}) collective-permute-start(bf16[1024,128]{1,0:T(8,128)(2,1)} %feat_hbm.1), channel_id=1, source_target_pairs={{0,4},{4,0},{8,12},{12,8},{16,20},{20,16},{24,28},{28,24},{32,36},... | collective-permute-start | bytes 786440 | tf_op jit(solution)/shard_map/ppermute | solution.py:277
  3.2 1.4 %collective-permute-start = (s32[12,256]{1,0:T(8,128)}, s32[12,256]{1,0:T(8,128)S(1)}, u32[]{:S(2)}, u32[]{:S(2)}) collective-permute-start(s32[12,256]{1,0:T(8,128)} %bitcast.8), channel_id=1, source_target_pairs={{0,4},{4,0},{8,12},{12,8},{16,20},{20,16},{24,28},{28,24},{32,36},... | collective-permute-start | bytes 36872 | tf_op jit(solution)/shard_map/ppermute | solution.py:276
  4.6 0.6 %copy-start.10 = (s32[12,256]{1,0:T(8,128)}, s32[12,256]{1,0:T(8,128)S(1)}, u32[]{:S(2)}) copy-start(s32[12,256]{1,0:T(8,128)S(1)} %collective-permute-done.other_hbm) | copy-start | bytes 36868
  4.6 0.7 %copy-start.9 = (bf16[1024,128]{1,0:T(8,128)(2,1)}, bf16[1024,128]{1,0:T(8,128)(2,1)S(1)}, u32[]{:S(2)}) copy-start(bf16[1024,128]{1,0:T(8,128)(2,1)S(1)} %collective-permute-done.1.near_feat_hbm) | copy-start | bytes 786436
  10.2 41.2 %all-to-all-start = ((bf16[128,32,128]{2,1,0:T(8,128)(2,1)}), bf16[128,32,128]{2,1,0:T(8,128)(2,1)S(1)}, u32[]{:S(2)}, u32[]{:S(2)}) async-start(bf16[128,32,128]{2,1,0:T(8,128)(2,1)} %bitcast.7), calls=%async_computation | async-start | bytes 2097152 | tf_op jit(solution)/shard_map/all_to_all | solution.py:279
  24.0 1.9 %copy-start.1 = (bf16[96,128,128]{2,1,0:T(8,128)(2,1)S(1)}, bf16[96,128,128]{2,1,0:T(8,128)(2,1)}, u32[]{:S(2)}) copy-start(bf16[96,128,128]{2,1,0:T(8,128)(2,1)} %values_ref.2) | copy-start | bytes 9437188
  25.9 0.9 %copy-start.3 = (bf16[1024,128]{1,0:T(8,128)(2,1)S(1)}, bf16[1024,128]{1,0:T(8,128)(2,1)}, u32[]{:S(2)}) copy-start(bf16[1024,128]{1,0:T(8,128)(2,1)} %get-tuple-element.12.mapped_ref) | copy-start | bytes 786436
  26.9 0.7 %copy-start.4 = (s32[96]{0:T(128)S(1)}, s32[96]{0:T(128)}, u32[]{:S(2)}) copy-start(s32[96]{0:T(128)} %rows_ref.2) | copy-start | bytes 1156
  27.5 0.7 %copy-start.5 = (s32[96]{0:T(128)S(1)}, s32[96]{0:T(128)}, u32[]{:S(2)}) copy-start(s32[96]{0:T(128)} %blocks_ref.2) | copy-start | bytes 1156
  28.2 0.7 %copy-start.6 = (f32[128]{0:T(128)S(1)}, f32[128]{0:T(128)}, u32[]{:S(2)}) copy-start(f32[128]{0:T(128)} %param.14) | copy-start | bytes 1540
  51.4 4.0 %copy-start.2 = (bf16[96,128,128]{2,1,0:T(8,128)(2,1)S(1)}, bf16[96,128,128]{2,1,0:T(8,128)(2,1)}, u32[]{:S(2)}) copy-start(bf16[96,128,128]{2,1,0:T(8,128)(2,1)} %values_ref.3) | copy-start | bytes 9437188
  51.4 4.0 %copy-start.7 = (s32[96]{0:T(128)S(1)}, s32[96]{0:T(128)}, u32[]{:S(2)}) copy-start(s32[96]{0:T(128)} %rows_ref.3) | copy-start | bytes 1156
  51.4 4.0 %copy-start.8 = (s32[96]{0:T(128)S(1)}, s32[96]{0:T(128)}, u32[]{:S(2)}) copy-start(s32[96]{0:T(128)} %blocks_ref.3) | copy-start | bytes 1156
  51.9 5.4 %copy-start = (bf16[1024,2048]{1,0:T(8,128)(2,1)S(1)}, bf16[1024,2048]{1,0:T(8,128)(2,1)}, u32[]{:S(2)}) copy-start(bf16[1024,2048]{1,0:T(8,128)(2,1)} %weights_ref.1) | copy-start | bytes 12582916
  51.9 5.4 %collective-permute-start.2 = (bf16[1024,128]{1,0:T(8,128)(2,1)S(1)}, bf16[1024,128]{1,0:T(8,128)(2,1)S(1)}, u32[]{:S(2)}, u32[]{:S(2)}) collective-permute-start(bf16[1024,128]{1,0:T(8,128)(2,1)S(1)} %get-tuple-element.16.own_ref), channel_id=1, source_target_pairs={{0,4},{4,0},{8,12},{12,8},{16,20},{20,16},{24,28},{28,24},{32,36},... | collective-permute-start | bytes 786440 | tf_op jit(solution)/shard_map/ppermute | solution.py:290
